TPU v7x, 256 devices: a whole 4x4x8 slice. The times are simulated.
256 devices in a mesh: fsdp: 64 (over z, x, core), rep: 4 (over y).
Axes of the slice: x: 4, y: 4, z: 8, core: 2. Of those that a mesh axis runs over, the one named last changes fastest.
Arguments:
- grads: bfloat16 [4, 3072, 18432], P('rep', 'fsdp'), may hold values from -0.59765625 to 0.59765625
- owner_map: int32 [4, 24], replicated, may hold values from 0 to 63, as said below
- stats_left: float32 [192, 768, 768], P('fsdp', 'rep'), may hold values from -1 to 8
- stats_right: float32 [192, 768, 768], P('fsdp', 'rep'), may hold values from -1 to 8
- roots_left: bfloat16 [192, 768, 768], P('fsdp', 'rep'), may hold values from -1 to 3, as said below
- roots_right: bfloat16 [192, 768, 768], P('fsdp', 'rep'), may hold values from -1 to 3, as said below
Outputs:
- new_left: float32 [192, 768, 768], P('fsdp', 'rep')
- new_right: float32 [192, 768, 768], P('fsdp', 'rep')
- update: bfloat16 [3072, 18432], P('fsdp')
Inputs may be any that keep to these rules, and one draw needn't show every extreme that they name: `owner_map`: no owner holds more than 3 blocks, and some owner holds exactly 3; no owner holds more than 1 block of one block row, and some owner holds exactly 1 of one row. `roots_left`: each entry is a symmetric matrix. `roots_right`: each entry is a symmetric matrix.
All inputs are finite; a program needn't handle non-finite values.
Results may differ from a plain program's by a relative error of at most 0.017.
Values may be sent and summed in bfloat16 or wider, within the bound.
A program may use at most 128 MiB of HBM per device.

v0:
```python
import jax
import jax.numpy as jnp
from jax import lax
from jax.sharding import PartitionSpec as P

stat_decay = 0.95


def block_tables(owner_map, own_index, slots):
    brows, bcols = owner_map.shape
    count = brows * bcols
    owners = owner_map.reshape(count)
    position = jnp.arange(count, dtype=jnp.int32)
    row_of = position // bcols
    same_owner = owners[:, None] == owners[None, :]
    before = position[None, :] < position[:, None]
    slot_of = jnp.sum((same_owner & before).astype(jnp.int32), axis=1)
    same_row = row_of[:, None] == row_of[None, :]
    rank_row = jnp.sum((same_owner & before & same_row).astype(jnp.int32), axis=1)
    slot_ids = jnp.arange(slots, dtype=jnp.int32)
    hits = (owners[None, :] == own_index) & (slot_of[None, :] == slot_ids[:, None])
    valid = jnp.any(hits, axis=1)
    slot_block = jnp.sum(jnp.where(hits, position[None, :], 0), axis=1)
    return (rank_row.reshape(brows, bcols), valid, slot_block // bcols, rank_row[slot_block])


def shards(grads, owner_map, stats_left, stats_right, roots_left, roots_right):
    fsdp_count = lax.axis_size("fsdp")
    own_index = lax.axis_index("fsdp")
    rep_index = lax.axis_index("rep")
    rows_dev = grads.shape[1]
    width = grads.shape[2]
    slots, band_rows, block = stats_left.shape
    brows, bcols = owner_map.shape
    group = block // rows_dev
    per_row = (slots + brows - 1) // brows
    ranks, valid, slot_row, slot_rank = block_tables(owner_map, own_index, slots)
    my_row = own_index // group
    owner_line = owner_map[my_row]
    rank_line = ranks[my_row]
    dest_ids = jnp.arange(fsdp_count, dtype=jnp.int32)
    piece_ids = jnp.arange(per_row, dtype=jnp.int32)
    column_ids = jnp.arange(bcols, dtype=jnp.int32)
    slot_ids = jnp.arange(slots, dtype=jnp.int32)
    send_hits = (owner_line[None, None, :] == dest_ids[:, None, None]) & (
        rank_line[None, None, :] == piece_ids[None, :, None]
    )
    send_index = jnp.where(
        jnp.any(send_hits, axis=2),
        jnp.sum(jnp.where(send_hits, column_ids[None, None, :], 0), axis=2),
        bcols,
    )
    partial_rows = grads[0].astype(jnp.float32)
    summed_rows = lax.psum(partial_rows.astype(jnp.bfloat16), "rep")
    height = summed_rows.shape[0]
    pieces = summed_rows.reshape(height, bcols, block).transpose(1, 0, 2)
    padded = jnp.concatenate([pieces, jnp.zeros((1, height, block), jnp.bfloat16)], axis=0)
    outgoing = padded[send_index]
    received = lax.all_to_all(outgoing, "fsdp", split_axis=0, concat_axis=0, tiled=True)
    shaped = received.reshape(brows, group, per_row, height, block)
    picked = shaped[slot_row, :, slot_rank]
    owned = picked.reshape(slots, block, block)
    owned_band = lax.dynamic_slice_in_dim(owned, rep_index * band_rows, band_rows, 1)
    owned_cols = lax.dynamic_slice_in_dim(owned, rep_index * band_rows, band_rows, 2)
    left_term = jnp.einsum("sik,sjk->sij", owned_band, owned, preferred_element_type=jnp.float32)
    right_term = jnp.einsum("ski,skj->sij", owned_cols, owned, preferred_element_type=jnp.float32)
    keep = valid[:, None, None]
    new_left = jnp.where(keep, stat_decay * stats_left + (1.0 - stat_decay) * left_term, stats_left)
    new_right = jnp.where(
        keep, stat_decay * stats_right + (1.0 - stat_decay) * right_term, stats_right
    )
    left_band = jnp.einsum(
        "sik,skj->sij", roots_left, owned, preferred_element_type=jnp.float32
    ).astype(jnp.bfloat16)
    right_full = lax.all_gather(roots_right, "rep", axis=1, tiled=True)
    finished_band = jnp.einsum(
        "sik,skj->sij", left_band, right_full, preferred_element_type=jnp.float32
    ).astype(jnp.bfloat16)
    finished = lax.all_gather(finished_band, "rep", axis=1, tiled=True)
    piece_width = finished.shape[2]
    dest_rows = dest_ids // group
    dest_parts = dest_ids % group
    back_hits = (
        valid[None, None, :]
        & (slot_row[None, None, :] == dest_rows[:, None, None])
        & (slot_rank[None, None, :] == piece_ids[None, :, None])
    )
    back_index = jnp.where(
        jnp.any(back_hits, axis=2),
        jnp.sum(jnp.where(back_hits, slot_ids[None, None, :], 0), axis=2),
        slots,
    )
    finished_pad = jnp.concatenate(
        [
            finished.reshape(slots, group, rows_dev, piece_width),
            jnp.zeros((1, group, rows_dev, piece_width), jnp.bfloat16),
        ],
        axis=0,
    )
    outgoing_back = finished_pad[back_index, dest_parts[:, None]]
    returned = lax.all_to_all(outgoing_back, "fsdp", split_axis=0, concat_axis=0, tiled=True)
    strip_pieces = returned[owner_line, rank_line]
    update = strip_pieces.transpose(1, 0, 2).reshape(rows_dev, width)
    return (new_left, new_right, update)


def solution(mesh):
    in_specs = (
        P("rep", "fsdp", None),
        P(),
        P("fsdp", "rep", None),
        P("fsdp", "rep", None),
        P("fsdp", "rep", None),
        P("fsdp", "rep", None),
    )
    out_specs = (P("fsdp", "rep", None), P("fsdp", "rep", None), P("fsdp", None))
    return jax.shard_map(shards, mesh=mesh, in_specs=in_specs, out_specs=out_specs, check_vma=False)
```

profile of v0, /device:TPU:1, one launch (start us, length us, event | category | flops | bytes accessed | tf_op | source)
XLA Modules:
  0.0 383.8 jit_solution(260372584256451825)
XLA Ops:
  7.2 0.0 all-reduce.4.cloned.1.call-start
  7.2 1.9 copy.33
  9.1 1.5 copy.35
  10.7 0.0 all-reduce.4.cloned.1.call-update
  10.7 0.1 broadcast_in_dim_reshape.2
  10.8 0.2 convert_reduce_fusion.1
  11.0 0.1 reshape.615
  11.1 0.1 select_reduce_fusion
  11.2 0.1 fusion.4
  11.3 62.1 %all-reduce.4.cloned.1.call-done = bf16[24,48,768]{2,1,0:T(8,128)(2,1)} async-done(((bf16[24,48,768]{2,1,0:T(8,128)(2,1)}), bf16[24,48,768]{2,1,0:T(8,128)(2,1)}) %all-reduce.4.cloned.1.call-update) | async-done | bytes 1769488 | tf_op jit(solution)/shard_map/psum | solution.py:54
  73.4 1.6 concatenate.15
  75.0 3.0 gather_fusion
  78.0 10.8 %all-to-all-start = ((bf16[64,1,48,768]{3,2,1,0:T(8,128)(2,1)}), bf16[64,1,48,768]{3,2,1,0:T(8,128)(2,1)}, u32[]{:S(2)}, u32[]{:S(2)}) async-start(bf16[64,1,48,768]{3,2,1,0:T(8,128)(2,1)} %bitcast.70), calls=%async_computation | async-start | bytes 9437184 | tf_op jit(solution)/shard_map/all_to_all | solution.py:59
  88.8 0.0 all-gather.3.cloned.1.call-start
  88.9 0.7 all-gather.3.cloned.1.call-update
  89.6 0.0 all-gather.5.cloned.1.call-start
  89.6 0.1 select_reduce_fusion.1
  89.8 0.6 gather_fusion.1
  90.4 103.6 %all-to-all-done = bf16[64,1,48,768]{3,2,1,0:T(8,128)(2,1)} async-done(((bf16[64,1,48,768]{3,2,1,0:T(8,128)(2,1)}), bf16[64,1,48,768]{3,2,1,0:T(8,128)(2,1)}, u32[]{:S(2)}, u32[]{:S(2)}) %all-to-all-start) | async-done | bytes 4718624 | tf_op jit(solution)/shard_map/all_to_all | solution.py:59
  194.1 5.0 %gather_fusion.2 = bf16[3,16,48,768]{3,2,1,0:T(8,128)(2,1)} fusion(bf16[4,16,1,48,768]{4,3,2,1,0:T(8,128)(2,1)} %bitcast.7, s32[3]{0:T(128)S(1)} %fusion.22), kind=kCustom, calls=%fused_computation.2 | custom fusion | bytes 7077912 | tf_op jit(solution)/shard_map/gather | solution.py:61
  199.0 5.5 %convolution_convert_fusion.1 = bf16[3,192,768]{2,1,0:T(8,128)(2,1)} fusion(bf16[3,768,768]{2,1,0:T(8,128)(2,1)} %all-gather.3.cloned.1.call-done, bf16[3,192,768]{2,1,0:T(8,128)(2,1)S(1)} %copy-done, bf16[3,768,768]{2,1,0:T(8,128)(2,1)} %bitcast.66), kind=kOutput, calls=%fused_computation.9 | convolution fusion | flops 1359839232 | bytes 8847360 | tf_op jit(solution)/shard_map/sik,skj->sij/dot_general | solution.py:76
  204.6 0.1 fusion.6
  204.8 0.1 select_reduce_fusion.2
  204.9 41.9 %all-gather.5.cloned.1.call-done = bf16[3,768,768]{2,1,0:T(8,128)(2,1)} async-done(((bf16[3,192,768]{2,1,0:T(8,128)(2,1)}), bf16[3,768,768]{2,1,0:T(8,128)(2,1)}) %all-gather.5.cloned.1.call-update) | async-done | bytes 3538960 | tf_op jit(solution)/shard_map/all_gather | solution.py:79
  246.8 4.5 %concatenate.17 = bf16[4,16,48,768]{3,2,1,0:T(8,128)(2,1)} pad(bf16[3,16,48,768]{3,2,1,0:T(8,128)(2,1)} %bitcast.74, bf16[]{:T(256)} %constant.80.clone.1), padding=0_1x0_0x0_0x0_0 | pad | bytes 8257538 | tf_op jit(solution)/shard_map/concatenate | solution.py:93
  251.4 5.3 %gather_fusion.3 = bf16[64,48,768]{2,1,0:T(8,128)(2,1)} fusion(bf16[4,16,48,768]{3,2,1,0:T(8,128)(2,1)} %concatenate.17, s32[64]{0:T(128)S(1)} %or_bitcast_fusion), kind=kCustom, calls=%fused_computation.3 | custom fusion | bytes 9437696 | tf_op jit(solution)/shard_map/gather | solution.py:100
  256.7 11.0 %all-to-all-start.1 = ((bf16[64,1,48,768]{3,2,1,0:T(8,128)(2,1)}), bf16[64,1,48,768]{3,2,1,0:T(8,128)(2,1)}, u32[]{:S(2)}, u32[]{:S(2)}) async-start(bf16[64,1,48,768]{3,2,1,0:T(8,128)(2,1)} %bitcast.69), calls=%async_computation.1 | async-start | bytes 9437184 | tf_op jit(solution)/shard_map/all_to_all | solution.py:101
  267.7 5.0 %add_select_fusion.1 = f32[3,192,768]{2,1,0:T(8,128)} fusion(f32[3,192,768]{2,1,0:T(8,128)S(1)} %copy-done.3, bf16[3,768,768]{2,1,0:T(8,128)(2,1)} %bitcast.67, s32[]{:T(128)S(6)} %select_n.231, pred[3]{0:T(512)(128)(4,1)S(1)} %fusion.6), kind=kOutput, calls=%fused_computation.7 | convolution fusion | flops 681246720 | bytes 7962631 | tf_op jit(solution)/shard_map/sik,sjk->sij/dot_general | solution.py:65
  272.7 2.6 add_select_fusion
  275.3 97.7 %all-to-all-done.1 = bf16[64,1,48,768]{3,2,1,0:T(8,128)(2,1)} async-done(((bf16[64,1,48,768]{3,2,1,0:T(8,128)(2,1)}), bf16[64,1,48,768]{3,2,1,0:T(8,128)(2,1)}, u32[]{:S(2)}, u32[]{:S(2)}) %all-to-all-start.1) | async-done | bytes 4718624 | tf_op jit(solution)/shard_map/all_to_all | solution.py:101
  372.9 3.0 gather_fusion.4
  375.9 1.3 copy.32
  (29 shorter events, 0.2 us)
Async XLA Ops:
  7.2 191.9 %copy-start = (bf16[3,192,768]{2,1,0:T(8,128)(2,1)S(1)}, bf16[3,192,768]{2,1,0:T(8,128)(2,1)}, u32[]{:S(2)}) copy-start(bf16[3,192,768]{2,1,0:T(8,128)(2,1)} %param.10) | copy-start | bytes 2654212
  7.2 66.2 %all-reduce.4.cloned.1.call-start = ((), (), s32[]{:S(2)}) async-start(), calls=%async_computation.2 | async-start | bytes 3538944 | tf_op jit(solution)/shard_map/psum | solution.py:54
  9.1 1.6 copy-start.4
  78.0 116.1 %all-to-all-start = ((bf16[64,1,48,768]{3,2,1,0:T(8,128)(2,1)}), bf16[64,1,48,768]{3,2,1,0:T(8,128)(2,1)}, u32[]{:S(2)}, u32[]{:S(2)}) async-start(bf16[64,1,48,768]{3,2,1,0:T(8,128)(2,1)} %bitcast.70), calls=%async_computation | async-start | bytes 9437184 | tf_op jit(solution)/shard_map/all_to_all | solution.py:59
  88.8 110.2 %all-gather.3.cloned.1.call-start = ((), (), s32[]{:S(2)}) async-start(), calls=%async_computation.3 | async-start | bytes 4423680 | tf_op jit(solution)/shard_map/all_gather | solution.py:75
  89.6 157.3 %all-gather.5.cloned.1.call-start = ((), (), s32[]{:S(2)}) async-start(), calls=%async_computation.4 | async-start | bytes 4423680 | tf_op jit(solution)/shard_map/all_gather | solution.py:79
  256.7 11.0 %copy-start.3 = (f32[3,192,768]{2,1,0:T(8,128)S(1)}, f32[3,192,768]{2,1,0:T(8,128)}, u32[]{:S(2)}) copy-start(f32[3,192,768]{2,1,0:T(8,128)} %param.8) | copy-start | bytes 5308420
  256.7 116.2 %all-to-all-start.1 = ((bf16[64,1,48,768]{3,2,1,0:T(8,128)(2,1)}), bf16[64,1,48,768]{3,2,1,0:T(8,128)(2,1)}, u32[]{:S(2)}, u32[]{:S(2)}) async-start(bf16[64,1,48,768]{3,2,1,0:T(8,128)(2,1)} %bitcast.69), calls=%async_computation.1 | async-start | bytes 9437184 | tf_op jit(solution)/shard_map/all_to_all | solution.py:101
  267.7 5.0 %copy-start.1 = (bf16[3,16,48,768]{3,2,1,0:T(8,128)(2,1)S(1)}, bf16[3,16,48,768]{3,2,1,0:T(8,128)(2,1)}, u32[]{:S(2)}) copy-start(bf16[3,16,48,768]{3,2,1,0:T(8,128)(2,1)} %gather_fusion.2) | copy-start | bytes 10616836
  267.7 5.0 %copy-start.2 = (f32[3,192,768]{2,1,0:T(8,128)S(1)}, f32[3,192,768]{2,1,0:T(8,128)}, u32[]{:S(2)}) copy-start(f32[3,192,768]{2,1,0:T(8,128)} %param.9) | copy-start | bytes 5308420
Sparse Core Ops, SparseCore 0:
  11.0 62.3 all-reduce.3
  91.6 44.7 all-gather.2
  204.7 42.0 all-gather.4
where the time goes:
time: 385 us; the launch traced here: 384 us
  waiting for transfers between devices  306 us (79%)
  local copies, waits for them, and re-layouts  28 us (7%)
  starting transfers between devices  21.9 us (6%)
  between operations  13.9 us (4%)
  matrix products  13.1 us (3%)
    all_to_all x1, waiting for transfers between devices, shards(): lax.all_to_all(outgoing, 'fsdp', split_axis=0, concat_axis=0, tiled=True)  104 us
    all_to_all x1, waiting for transfers between devices, shards(): lax.all_to_all(outgoing_back, 'fsdp', split_axis=0, concat_axis=0, tiled=...  97.7 us
    psum x1, waiting for transfers between devices, shards(): summed_rows = lax.psum(partial_rows.astype(jnp.bfloat16), 'rep')  62.1 us
    all_gather x1, waiting for transfers between devices, shards(): finished = lax.all_gather(finished_band, 'rep', axis=1, tiled=True)  41.9 us
    all_to_all x1, starting transfers between devices, shards(): lax.all_to_all(outgoing_back, 'fsdp', split_axis=0, concat_axis=0, tiled=...  11 us
    all_to_all x1, starting transfers between devices, shards(): lax.all_to_all(outgoing, 'fsdp', split_axis=0, concat_axis=0, tiled=True)  10.8 us
  transfers between devices with their start and end apart: 5, of which 4 were waited for; matrix products, arithmetic and copies ran while one was open for 4% of the time, Pallas kernels for 0%

commit v1 on v0

v1 whole, which is shorter than its diff:
```python
import jax
import jax.numpy as jnp
from jax import lax
from jax.experimental import pallas as pl
from jax.experimental.pallas import tpu as pltpu
from jax.sharding import PartitionSpec as P

stat_decay = 0.95
MESH = pl.DeviceIdType.MESH
LANES = 128
TALL = 48
PIECE = 80
BF16 = jnp.bfloat16
F32 = jnp.float32


def kernel(
    own, g_hbm, sl_hbm, sr_hbm, rl_hbm, rr_hbm,
    nl_hbm, nr_hbm, up_hbm,
    g_v, pk, rs_rel, rs_dir, rs_acc, rs_out, strip,
    out, ro, ri, rrel, turned, gi, G, GT,
    uo, rb, ag, to, ti, trel,
    sl_v, sr_v, rl_v, rr_v, up_v, jtbl, stbl,
    load_sem, copy_sem, store_sem, plane_sem, cube_sem,
    rs_s, rs_r, a_s, a_r, ro_s, ro_r, b_s, b_r, t_s, t_r, ag_s, ag_r,
):
    f = lax.axis_index("fsdp")
    q = lax.axis_index("rep")
    nf = lax.axis_size("fsdp")
    brows, bcols = own.shape
    group = nf // brows
    block = G.shape[0]
    slots, band, _ = sl_v.shape
    half = bcols // 2
    up, dn, opp = lax.rem(q + 1, 4), lax.rem(q + 3, 4), lax.rem(q + 2, 4)
    fi, fk = f // group, lax.rem(f, group)

    def rcopy(src, dst, ssem, rsem, rep):
        return pltpu.make_async_remote_copy(
            src_ref=src, dst_ref=dst, send_sem=ssem, recv_sem=rsem,
            device_id=(f, rep), device_id_type=MESH,
        )

    loads = [
        pltpu.make_async_copy(src, dst, load_sem.at[n])
        for n, (src, dst) in enumerate(
            [(g_hbm.at[0], g_v), (rl_hbm, rl_v), (rr_hbm, rr_v), (sl_hbm, sl_v), (sr_hbm, sr_v)]
        )
    ]
    for load in loads:
        load.start()

    def shift(o):
        return lax.rem(2 * lax.rem(o, 2) + lax.rem(o // 2, 4) + o // 8, 4)

    my_shift = shift(f)
    site_row = lax.rem(q + 4 - my_shift, 4)
    own_row = site_row == fi

    plane0 = (f // 8) * 8
    z_line = [(lax.rem(f + 8 * n, nf), q) for n in range(1, nf // 8)]
    x_line = [(plane0 + lax.rem(f + n, 8), q) for n in range(1, 8)]
    y_line = [(f, lax.rem(q + n, 4)) for n in range(1, 4)]

    def greet(sem, devices):
        for device in devices:
            pl.semaphore_signal(sem, inc=1, device_id=device, device_id_type=MESH)

    barrier = pltpu.get_barrier_semaphore()
    greet(barrier, y_line + x_line + z_line)

    def extra(t):
        return (0 if t < 2 else 16), 4 + t % 2

    loads[0].wait()

    def pack(j, carry):
        base = j * block
        for t in range(4):
            row, lane = extra(t)
            pk[t, j, 0:TALL, :] = g_v[:, pl.ds(pl.multiple_of(base + t * LANES, LANES), LANES)]
            pk[t, j, TALL:PIECE, :] = g_v[
                row : row + 32, pl.ds(pl.multiple_of(base + lane * LANES, LANES), LANES)
            ]
        return carry

    lax.fori_loop(0, bcols, pack, 0)
    pl.semaphore_wait(barrier, len(y_line) + len(x_line) + len(z_line))

    lo, hi = pl.ds(0, half), pl.ds(half, half)
    rs = [
        rcopy(pk.at[opp, lo], rs_rel.at[0], rs_s.at[0], rs_r.at[0], dn),
        rcopy(pk.at[opp, hi], rs_rel.at[1], rs_s.at[1], rs_r.at[1], up),
        rcopy(pk.at[up, lo], rs_dir.at[0], rs_s.at[2], rs_r.at[2], up),
        rcopy(pk.at[dn, hi], rs_dir.at[1], rs_s.at[3], rs_r.at[3], dn),
        rcopy(rs_out.at[0], rs_acc.at[0], rs_s.at[4], rs_r.at[4], dn),
        rcopy(rs_out.at[1], rs_acc.at[1], rs_s.at[5], rs_r.at[5], up),
    ]
    for copy in rs[:4]:
        copy.start()
    greet(plane_sem, x_line)

    def column_of(o, carry):
        col = jnp.int32(0)
        for j in range(bcols):
            col = jnp.where(own[fi, j] == o, jnp.int32(j), col)
        jtbl[o] = col
        return carry

    lax.fori_loop(0, nf, column_of, 0)
    held = []
    for t in range(brows):
        count = jnp.int32(0)
        for j in range(bcols):
            count = count + jnp.where(own[t, j] == f, jnp.int32(1), jnp.int32(0))
        held.append(count)
    before = jnp.int32(0)
    for t in range(brows):
        stbl[t] = jnp.minimum(before, slots - 1)
        before = before + held[t]
    slot_row, slot_valid = [], []
    for s in range(slots):
        row, valid = jnp.int32(0), jnp.int32(0)
        before = jnp.int32(0)
        for t in range(brows):
            hit = jnp.where(before == s, held[t], 0)
            row = row + hit * t
            valid = valid + hit
            before = before + held[t]
        slot_row.append(row)
        slot_valid.append(valid)

    loads[1].wait()
    loads[2].wait()
    for t in range(4):
        slot = stbl[lax.rem(t + 4 - my_shift, 4)]
        ro[t, 0] = rl_v[slot]
        ro[t, 1] = rr_v[slot]
    pl.semaphore_wait(plane_sem, len(x_line))
    greet(cube_sem, y_line)

    def relay_sum(n, first, target):
        def body(j, carry):
            rs_out[n, j] = (rs_rel[n, j].astype(F32) + pk[target, first + j].astype(F32)).astype(BF16)
            return carry

        lax.fori_loop(0, half, body, 0)

    rs[0].wait_recv()
    relay_sum(0, 0, dn)
    rs[4].start()
    rs[1].wait_recv()
    relay_sum(1, half, up)
    rs[5].start()

    def full_sum(n, first):
        def body(j, carry):
            strip[first + j] = (
                pk[q, first + j].astype(F32) + rs_dir[n, j].astype(F32) + rs_acc[n, j].astype(F32)
            ).astype(BF16)
            return carry

        lax.fori_loop(0, half, body, 0)

    rs[2].wait_recv()
    rs[4].wait_recv()
    full_sum(0, 0)
    rs[3].wait_recv()
    rs[5].wait_recv()
    full_sum(1, half)

    pl.semaphore_wait(cube_sem, len(y_line))

    def piece_copy(o):
        return pltpu.make_async_remote_copy(
            src_ref=out.at[o], dst_ref=gi.at[q, fk], send_sem=a_s, recv_sem=a_r,
            device_id=(o, lax.rem(fi + shift(o), 4)), device_id_type=MESH,
        )

    def send_piece(d, carry):
        o = lax.rem(f + d, nf)
        out[o] = strip[jtbl[o]]
        piece_copy(o).start()
        return carry

    lax.fori_loop(1, nf, send_piece, 0)

    @pl.when(own_row)
    def _():
        gi[q, fk] = strip[jtbl[f]]

    @pl.when(jnp.logical_not(own_row))
    def _():
        out[f] = strip[jtbl[f]]
        piece_copy(f).start()

    def await_pieces(sem):
        def some(count):
            view = out.at[pl.ds(0, count)]
            pltpu.make_async_copy(view, view, sem).wait()

        pl.when(own_row)(lambda: some(nf - 1))
        pl.when(jnp.logical_not(own_row))(lambda: some(nf))

    def exchange(far, outs, ins, far_ins, rel, ssem, rsem):
        return [
            rcopy(far[0], rel.at[0], ssem.at[0], rsem.at[0], dn),
            rcopy(far[1], rel.at[1], ssem.at[1], rsem.at[1], up),
            rcopy(outs.at[up], ins.at[q], ssem.at[2], rsem.at[2], up),
            rcopy(outs.at[dn], ins.at[q], ssem.at[3], rsem.at[3], dn),
            rcopy(rel.at[0], far_ins[0], ssem.at[4], rsem.at[4], dn),
            rcopy(rel.at[1], far_ins[1], ssem.at[5], rsem.at[5], up),
        ]

    def begin(copies, own_copy):
        for copy in copies[:4]:
            copy.start()
        own_copy.start()

    def forward(copies):
        copies[0].wait_recv()
        copies[4].start()
        copies[1].wait_recv()
        copies[5].start()

    def finish(copies, own_copy):
        for copy in copies[2:]:
            copy.wait_recv()
        own_copy.wait()

    def window(t):
        return pl.ds(pl.multiple_of(LANES * (t + t // 2), LANES), 2 * LANES)

    roots = exchange(
        [ro.at[opp, n, :, window(q)] for n in range(2)], ro, ri,
        [ri.at[up, 0, :, window(up)], ri.at[dn, 1, :, window(dn)]], rrel, ro_s, ro_r,
    )
    roots_own = pltpu.make_async_copy(ro.at[q], ri.at[q], copy_sem.at[0])
    begin(roots, roots_own)
    forward(roots)
    finish(roots, roots_own)
    for n in range(2):
        turned[...] = ri[:, n, :, window(opp)].reshape(block, 2 * LANES).T
        ri[opp, n] = turned[pl.ds(pl.multiple_of(64 * lax.rem(opp, 2), 16), band), :]

    await_pieces(a_r)

    def unpack_block(k, carry):
        row0 = pl.multiple_of(k * TALL, 16)
        for t in range(4):
            row, lane = extra(t)
            G[pl.ds(row0, TALL), t * LANES : (t + 1) * LANES] = gi[t, k, 0:TALL, :]
            skip = 0 if t < 2 else 16
            G[pl.ds(pl.multiple_of(row0 + row + skip, 16), 32 - skip), lane * LANES : (lane + 1) * LANES] = gi[
                t, k, TALL + skip : PIECE, :
            ]
        return carry

    lax.fori_loop(0, group, unpack_block, 0)

    per_band = band // TALL

    def precondition(c, carry):
        p = jnp.dot(ri[c, 0], G[...], preferred_element_type=F32).astype(BF16)
        u = jnp.dot(p, ri[:, 1].reshape(block, block), preferred_element_type=F32).astype(BF16)
        for n in range(per_band):
            k = c * per_band + n
            for t in range(4):
                row, lane = extra(t)
                uo[t, k, 0:TALL, :] = u[n * TALL : (n + 1) * TALL, t * LANES : (t + 1) * LANES]
                uo[t, k, TALL:PIECE, :] = u[
                    n * TALL + row : n * TALL + row + 32, lane * LANES : (lane + 1) * LANES
                ]
        return carry

    lax.fori_loop(0, 4, precondition, 0)

    def piece_back(e):
        t, k = lax.rem(e, 4), lax.rem(e // 4 + fk, group)
        p = site_row * group + k
        copy = pltpu.make_async_remote_copy(
            src_ref=uo.at[t, k], dst_ref=rb.at[f], send_sem=b_s, recv_sem=b_r,
            device_id=(p, t), device_id_type=MESH,
        )
        return copy, jnp.logical_and(p == f, t == q)

    def send_back(e, carry):
        copy, here = piece_back(e)

        @pl.when(jnp.logical_not(here))
        def _():
            copy.start()

        return carry

    lax.fori_loop(0, nf, send_back, 0)

    @pl.when(own_row)
    def _():
        rb[f] = uo[q, fk]

    GT[...] = G[...].T

    def products_left(c, carry):
        rows = G[pl.ds(pl.multiple_of(c * band, 16), band), :]
        to[c, 0] = lax.dot_general(
            rows, G[...], (((1,), (1,)), ((), ())), preferred_element_type=F32
        ).astype(BF16)
        return carry

    def products_right(c, carry):
        rows = GT[pl.ds(pl.multiple_of(c * band, 16), band), :]
        to[c, 1] = jnp.dot(rows, G[...], preferred_element_type=F32).astype(BF16)
        return carry

    lax.fori_loop(0, 4, products_left, 0)
    lax.fori_loop(0, 4, products_right, 0)

    stats = exchange(
        [to.at[opp, 0], to.at[opp, 1]], to, ti, [ti.at[up, 0], ti.at[dn, 1]], trel, t_s, t_r
    )
    stats_own = pltpu.make_async_copy(to.at[q], ti.at[q], copy_sem.at[1])
    begin(stats, stats_own)
    forward(stats)
    finish(stats, stats_own)
    loads[3].wait()
    loads[4].wait()
    for s in range(slots):
        for n, ref in ((0, sl_v), (1, sr_v)):
            old = ref[s]
            term = ti[lax.rem(slot_row[s] + my_shift, 4), n].astype(F32)
            ref[s] = jnp.where(slot_valid[s] > 0, stat_decay * old + (1.0 - stat_decay) * term, old)
    stores = [
        pltpu.make_async_copy(sl_v, nl_hbm, store_sem.at[0]),
        pltpu.make_async_copy(sr_v, nr_hbm, store_sem.at[1]),
        pltpu.make_async_copy(up_v, up_hbm, store_sem.at[2]),
    ]
    stores[0].start()
    stores[1].start()

    await_pieces(b_r)

    def pick(j, carry):
        ag[q, j] = rb[own[fi, j]]
        return carry

    lax.fori_loop(0, bcols, pick, 0)
    gather = [
        rcopy(ag.at[q], ag.at[q], ag_s.at[0], ag_r.at[0], up),
        rcopy(ag.at[q], ag.at[q], ag_s.at[1], ag_r.at[1], dn),
        rcopy(ag.at[up, lo], ag.at[up, lo], ag_s.at[2], ag_r.at[2], dn),
        rcopy(ag.at[dn, hi], ag.at[dn, hi], ag_s.at[3], ag_r.at[3], up),
    ]
    gather[0].start()
    gather[1].start()
    gather[1].wait_recv()
    gather[2].start()
    gather[0].wait_recv()
    gather[3].start()
    gather[2].wait_recv()
    gather[3].wait_recv()

    def unpack_row(j, carry):
        base = j * block
        for t in range(4):
            row, lane = extra(t)
            skip = 0 if t < 2 else 16
            up_v[:, pl.ds(pl.multiple_of(base + t * LANES, LANES), LANES)] = ag[t, j, 0:TALL, :]
            up_v[row + skip : row + 32, pl.ds(pl.multiple_of(base + lane * LANES, LANES), LANES)] = ag[
                t, j, TALL + skip : PIECE, :
            ]
        return carry

    lax.fori_loop(0, bcols, unpack_row, 0)
    stores[2].start()

    for copies in (rs, roots, stats, gather):
        for copy in copies:
            copy.wait_send()
    await_pieces(a_s)
    await_pieces(b_s)
    for store in stores:
        store.wait()


def shards(grads, owner_map, stats_left, stats_right, roots_left, roots_right):
    _, rows, width = grads.shape
    slots, band, block = stats_left.shape
    brows, bcols = owner_map.shape
    nf = lax.axis_size("fsdp")
    group = nf // brows
    half = bcols // 2
    dma, reg = pltpu.SemaphoreType.DMA, pltpu.VMEM
    msg = (PIECE, LANES)
    scratch = [
        reg((rows, width), BF16),
        reg((4, bcols) + msg, BF16),
        reg((2, half) + msg, BF16),
        reg((2, half) + msg, BF16),
        reg((2, half) + msg, BF16),
        reg((2, half) + msg, BF16),
        reg((bcols,) + msg, BF16),
        reg((nf,) + msg, BF16),
        reg((4, 2, band, block), BF16),
        reg((4, 2, band, block), BF16),
        reg((2, band, 2 * LANES), BF16),
        reg((2 * LANES, block), BF16),
        reg((4, group) + msg, BF16),
        reg((block, block), BF16),
        reg((block, block), BF16),
        reg((4, group) + msg, BF16),
        reg((nf,) + msg, BF16),
        reg((4, bcols) + msg, BF16),
        reg((4, 2, band, block), BF16),
        reg((4, 2, band, block), BF16),
        reg((2, band, block), BF16),
        reg((slots, band, block), F32),
        reg((slots, band, block), F32),
        reg((slots, band, block), BF16),
        reg((slots, band, block), BF16),
        reg((rows, width), BF16),
        pltpu.SMEM((nf,), jnp.int32),
        pltpu.SMEM((brows,), jnp.int32),
        dma((5,)), dma((2,)), dma((3,)), pltpu.SemaphoreType.REGULAR, pltpu.SemaphoreType.REGULAR,
        dma((6,)), dma((6,)), dma, dma, dma((6,)), dma((6,)),
        dma, dma, dma((6,)), dma((6,)), dma((4,)), dma((4,)),
    ]
    hbm = pl.BlockSpec(memory_space=pl.ANY)
    return pl.pallas_call(
        kernel,
        out_shape=(
            jax.ShapeDtypeStruct(stats_left.shape, F32),
            jax.ShapeDtypeStruct(stats_right.shape, F32),
            jax.ShapeDtypeStruct((rows, width), BF16),
        ),
        in_specs=[pl.BlockSpec(memory_space=pltpu.SMEM)] + [hbm] * 5,
        out_specs=(hbm, hbm, hbm),
        scratch_shapes=scratch,
        compiler_params=pltpu.CompilerParams(
            collective_id=0, has_side_effects=True, vmem_limit_bytes=60 * 1024 * 1024
        ),
        name="shampoo",
    )(owner_map, grads, stats_left, stats_right, roots_left, roots_right)


def solution(mesh):
    in_specs = (
        P("rep", "fsdp", None),
        P(),
        P("fsdp", "rep", None),
        P("fsdp", "rep", None),
        P("fsdp", "rep", None),
        P("fsdp", "rep", None),
    )
    out_specs = (P("fsdp", "rep", None), P("fsdp", "rep", None), P("fsdp", None))
    return jax.shard_map(shards, mesh=mesh, in_specs=in_specs, out_specs=out_specs, check_vma=False)
```

time: 385 us -> 140 us (0.36)
  waiting for transfers between devices: 306 us -> 0 us
  Pallas kernels: 0 us -> 132 us
  starting transfers between devices: 21.9 us -> 0 us
  local copies, waits for them, and re-layouts: 28 us -> 6.25 us
  between operations: 13.9 us -> 0.65 us
  matrix products: 13.1 us -> 0 us
    all_to_all x2 -> x0, waiting for transfers between devices: 201 us -> none  [the longest x1 104 us: shards(): lax.all_to_all(outgoing, 'fsdp', split_axis=0, concat_axis=0, tiled=True)]
    pallas_call x0 -> x1, Pallas kernels: none -> 132 us  [shards(): pl.pallas_call(kernel, out_shape=(jax.ShapeDtypeStruct(stats_left.shape,...]
    psum x1 -> x0, waiting for transfers between devices: 62.1 us -> none  [shards(): summed_rows = lax.psum(partial_rows.astype(jnp.bfloat16), 'rep')]
    all_gather x2 -> x0, waiting for transfers between devices: 41.9 us -> none  [the longest x1 41.9 us: shards(): finished = lax.all_gather(finished_band, 'rep', axis=1, tiled=True)]
    all_to_all x2 -> x0, starting transfers between devices: 21.8 us -> none  [the longest x1 11 us: shards(): lax.all_to_all(outgoing_back, 'fsdp', split_axis=0, concat_axis=0, tiled=...]
    gather x5 -> x0, local copies, waits for them, and re-layouts: 16.9 us -> none  [the longest x1 5.31 us: shards(): outgoing_back = finished_pad[back_index, dest_parts[:, None]]]
    dot_general x3 -> x0, matrix products: 13.1 us -> none  [the longest x1 5.55 us: shards(): jnp.einsum('sik,skj->sij', left_band, right_full, preferred_element_type=...]
    concatenate x2 -> x0, local copies, waits for them, and re-layouts: 6.13 us -> none  [the longest x1 4.54 us: shards(): jnp.concatenate([finished.reshape(slots, group, rows_dev, piece_width), j...]
  transfers between devices with their start and end apart: 5 -> 0, of which waited for: 4 -> 0; matrix products, arithmetic and copies ran while one was open for 4% -> 0% of each run, Pallas kernels for 0% -> 0%
where the time goes in v1:
time: 140 us; the launch traced here: 139 us
  Pallas kernels  132 us (94%)
  local copies, waits for them, and re-layouts  6.25 us (4%)
    pallas_call x1, Pallas kernels, shards(): pl.pallas_call(kernel, out_shape=(jax.ShapeDtypeStruct(stats_left.shape,...  132 us
    unnamed x7, local copies, waits for them, and re-layouts  6.25 us

profile of v1, /device:TPU:1, one launch (start us, length us, event | category | flops | bytes accessed | tf_op | source)
XLA Modules:
  0.0 139.0 jit_solution(16442506099486115237)
XLA Ops:
  0.6 132.1 %shampoo.1 = (f32[3,192,768]{2,1,0:T(8,128)}, f32[3,192,768]{2,1,0:T(8,128)}, bf16[48,18432]{1,0:T(8,128)(2,1)}) custom-call(s32[4,24]{1,0:T(4,128)} %own.1, bf16[1,48,18432]{2,1,0:T(8,128)(2,1)} %g_hbm.1, f32[3,192,768]{2,1,0:T(8,128)} %sl_hbm.1, f32[3,192,768]{2,1,0:T(8,128)} %sr_hbm.1, bf16[3,192,768]{2,1,0:T(8,128)(2,1)} %rl_hbm.1, ...), custom_call_target="tpu_custom_call" | custom-call | tf_op jit(solution)/shard_map/shampoo/pallas_call | solution.py:429
  132.8 0.0 copy-start.1
  132.8 2.9 %copy.12 = f32[3,192,768]{2,1,0:T(8,128)} copy(f32[3,192,768]{2,1,0:T(8,128)} %get-tuple-element.6) | data formatting | bytes 3538944
  135.7 0.0 copy-done.1
  135.7 0.0 copy-start
  135.7 1.2 copy.13
  136.9 0.9 copy-done
  137.8 1.2 copy.14
Async XLA Ops:
  132.8 2.9 %copy-start.1 = (f32[3,192,768]{2,1,0:T(8,128)S(1)}, f32[3,192,768]{2,1,0:T(8,128)}, u32[]{:S(2)}) copy-start(f32[3,192,768]{2,1,0:T(8,128)} %get-tuple-element.7) | copy-start | bytes 5308420
  135.7 2.1 %copy-start = (bf16[48,18432]{1,0:T(8,128)(2,1)S(1)}, bf16[48,18432]{1,0:T(8,128)(2,1)}, u32[]{:S(2)}) copy-start(bf16[48,18432]{1,0:T(8,128)(2,1)} %get-tuple-element.8) | copy-start | bytes 5308420

commit v2 on v1

v2 whole, which is shorter than its diff:
```python
import jax
import jax.numpy as jnp
from jax import lax
from jax.experimental import pallas as pl
from jax.experimental.pallas import tpu as pltpu
from jax.sharding import PartitionSpec as P

stat_decay = 0.95
MESH = pl.DeviceIdType.MESH
LANES = 128
TALL = 48
PIECE = 80
CHUNKS = ((0, 32), (32, 32), (64, 16))
BF16 = jnp.bfloat16
F32 = jnp.float32


class Copy:
    def __init__(self, copy, sends=None, receives=None):
        self.copy, self.sends, self.receives = copy, sends, receives

    def start(self):
        gated(self.sends, self.copy.start)

    def wait_send(self):
        gated(self.sends, self.copy.wait_send)

    def wait_recv(self):
        gated(self.receives, self.copy.wait_recv)


def gated(condition, act):
    if condition is None:
        act()
    else:

        @pl.when(condition)
        def _():
            act()


def kernel(
    own, g_hbm, sl_hbm, sr_hbm, rl_hbm, rr_hbm,
    nl_hbm, nr_hbm, up_hbm,
    g_v, pk, rs_rel, rs_dir, rs_acc, rs_out, strip,
    out, ro, ri, rrel, turned, gi, G, GT,
    uo, rb0, rb1, rb2, ag, to, ti, trel,
    sl_v, sr_v, rl_v, rr_v, up_v, jtbl, stbl,
    load_sem, copy_sem, store_sem, near_sem, line_sem, plane_sem, cube_sem,
    rs_s, rs_r, a_s, a_r, ro_s, ro_r, b_s, b_r, t_s, t_r, ag_s, ag_r,
):
    f = lax.axis_index("fsdp")
    q = lax.axis_index("rep")
    nf = lax.axis_size("fsdp")
    brows, bcols = own.shape
    group = nf // brows
    block = G.shape[0]
    slots, band, _ = sl_v.shape
    half = bcols // 2
    up, dn, opp = lax.rem(q + 1, 4), lax.rem(q + 3, 4), lax.rem(q + 2, 4)
    fi, fk, core = f // group, lax.rem(f, group), lax.rem(f, 2)

    def rcopy(src, dst, ssem, rsem, rep, sends=None, receives=None):
        copy = pltpu.make_async_remote_copy(
            src_ref=src, dst_ref=dst, send_sem=ssem, recv_sem=rsem,
            device_id=(f, rep), device_id_type=MESH,
        )
        return Copy(copy, sends, receives)

    loads = [
        pltpu.make_async_copy(src, dst, load_sem.at[n])
        for n, (src, dst) in enumerate(
            [(g_hbm.at[0], g_v), (rl_hbm, rl_v), (rr_hbm, rr_v), (sl_hbm, sl_v), (sr_hbm, sr_v)]
        )
    ]

    def shift(o):
        return lax.rem(2 * lax.rem(o, 2) + lax.rem(o // 2, 4) + o // 8, 4)

    my_shift = shift(f)
    site_row = lax.rem(q + 4 - my_shift, 4)
    own_row = site_row == fi

    def along_z(n):
        return (lax.rem(f + 8 * n, nf), q)

    def along_x(n):
        return ((f // 8) * 8 + lax.rem(f + n, 8), q)

    near = [along_z(1), along_z(7), along_x(1), along_x(7)]
    further = [along_z(2), along_z(6), along_x(2), along_x(6)]
    x_line = [along_x(n) for n in range(1, 8)]
    y_line = [(f, up), (f, dn), (f, opp)]

    def greet(sem, devices):
        for device in devices:
            pl.semaphore_signal(sem, inc=1, device_id=device, device_id_type=MESH)

    loads[0].start()
    barrier = pltpu.get_barrier_semaphore()
    greet(barrier, y_line + near)
    for load in loads[1:]:
        load.start()

    def column_of(o, carry):
        col = jnp.int32(0)
        for j in range(bcols):
            col = jnp.where(own[fi, j] == o, jnp.int32(j), col)
        jtbl[o] = col
        return carry

    lax.fori_loop(0, nf, column_of, 0)
    held = []
    for t in range(brows):
        count = jnp.int32(0)
        for j in range(bcols):
            count = count + jnp.where(own[t, j] == f, jnp.int32(1), jnp.int32(0))
        held.append(count)
    before = jnp.int32(0)
    for t in range(brows):
        stbl[t] = jnp.minimum(before, slots - 1)
        before = before + held[t]
    slot_row, slot_valid = [], []
    for s in range(slots):
        row, valid = jnp.int32(0), jnp.int32(0)
        before = jnp.int32(0)
        for t in range(brows):
            hit = jnp.where(before == s, held[t], 0)
            row = row + hit * t
            valid = valid + hit
            before = before + held[t]
        slot_row.append(row)
        slot_valid.append(valid)

    def tall(t, c):
        return lax.rem(t + 2 * c, 4) < 2

    tall_q, tall_up, tall_dn, tall_opp = [tall(t, core) for t in (q, up, dn, opp)]

    def lanes(base, group_of):
        return pl.ds(pl.multiple_of(base + group_of * LANES, LANES), LANES)

    loads[0].wait()

    def pack(j, carry):
        base = j * block
        for t in range(4):
            pk[t, j, 0:TALL, :] = g_v[:, lanes(base, t)]
        for t in range(2):
            pk[t + 2 * core, j, TALL:PIECE, :] = g_v[0:32, lanes(base, 4 + t)]
            pk[t + 2 * (1 - core), j, TALL:64, :] = g_v[32:TALL, lanes(base, 4 + t)]
        return carry

    lax.fori_loop(0, bcols, pack, 0)
    pl.semaphore_wait(barrier, len(y_line) + len(near))

    def sums(n):
        row, count = CHUNKS[n]
        lo, hi, rows = pl.ds(0, half), pl.ds(half, half), pl.ds(row, count)
        if n < 2:
            s_up = s_dn = s_opp = r_up = r_dn = r_q = None
        else:
            s_up, s_dn, s_opp, r_up, r_dn, r_q = tall_up, tall_dn, tall_opp, tall_up, tall_dn, tall_q
        ss, rr = rs_s.at[n], rs_r.at[n]
        return [
            rcopy(pk.at[opp, lo, rows], rs_rel.at[0, :, rows], ss.at[0], rr.at[0], dn, s_opp, r_dn),
            rcopy(pk.at[opp, hi, rows], rs_rel.at[1, :, rows], ss.at[1], rr.at[1], up, s_opp, r_up),
            rcopy(pk.at[up, lo, rows], rs_dir.at[0, :, rows], ss.at[2], rr.at[2], up, s_up, r_q),
            rcopy(pk.at[dn, hi, rows], rs_dir.at[1, :, rows], ss.at[3], rr.at[3], dn, s_dn, r_q),
            rcopy(rs_out.at[0, :, rows], rs_acc.at[0, :, rows], ss.at[4], rr.at[4], dn, s_dn, r_q),
            rcopy(rs_out.at[1, :, rows], rs_acc.at[1, :, rows], ss.at[5], rr.at[5], up, s_up, r_q),
        ]

    rs = [sums(n) for n in range(3)]

    def first_sends(n):
        for copy in rs[n][:4]:
            copy.start()

    def relay_sums(n):
        row, count = CHUNKS[n]
        rows = slice(row, row + count)
        for side, first, target in ((0, 0, dn), (1, half, up)):
            rs[n][side].wait_recv()

            def body(j, carry):
                total = rs_rel[side, j, rows].astype(F32) + pk[target, first + j, rows].astype(F32)
                rs_out[side, j, rows] = total.astype(BF16)
                return carry

            lax.fori_loop(0, half, body, 0)
            rs[n][4 + side].start()

    def full_sums(n):
        row, count = CHUNKS[n]
        rows = slice(row, row + count)
        for side, first in ((0, 0), (1, half)):
            rs[n][2 + side].wait_recv()
            rs[n][4 + side].wait_recv()

            def body(j, carry):
                total = pk[q, first + j, rows].astype(F32) + rs_dir[side, j, rows].astype(F32)
                strip[first + j, rows] = (total + rs_acc[side, j, rows].astype(F32)).astype(BF16)
                return carry

            lax.fori_loop(0, half, body, 0)

    def send_pieces(n):
        row, count = CHUNKS[n]
        rows = pl.ds(row, count)

        def piece_copy(o):
            return pltpu.make_async_remote_copy(
                src_ref=out.at[o, rows], dst_ref=gi.at[q, fk, rows], send_sem=a_s.at[n], recv_sem=a_r.at[n],
                device_id=(o, lax.rem(fi + shift(o), 4)), device_id_type=MESH,
            )

        def send_piece(d, carry):
            o = lax.rem(f + d, nf)
            out[o, row : row + count] = strip[jtbl[o], row : row + count]
            piece_copy(o).start()
            return carry

        def send_all():
            lax.fori_loop(1, nf, send_piece, 0)

            @pl.when(own_row)
            def _():
                gi[q, fk, row : row + count] = strip[jtbl[f], row : row + count]

            @pl.when(jnp.logical_not(own_row))
            def _():
                out[f, row : row + count] = strip[jtbl[f], row : row + count]
                piece_copy(f).start()

        gated(None if n < 2 else tall_q, send_all)

    def await_pieces(sem, n, total, here):
        count = CHUNKS[n][1]

        def some(pieces):
            view = out.at[pl.ds(0, pieces), pl.ds(0, count)]
            pltpu.make_async_copy(view, view, sem.at[n]).wait()

        pl.when(here)(lambda: some(total - 1))
        pl.when(jnp.logical_not(here))(lambda: some(total))

    def await_strip(sem, n):
        gated(None if n < 2 else tall_q, lambda: await_pieces(sem, n, nf, own_row))

    def await_block(sem, n):
        if n < 2:
            await_pieces(sem, n, nf, own_row)
        else:
            await_pieces(sem, n, nf // 2, jnp.logical_and(own_row, tall_q))

    def exchange(far, outs, ins, far_ins, rel, ssem, rsem):
        return [
            rcopy(far[0], rel.at[0], ssem.at[0], rsem.at[0], dn),
            rcopy(far[1], rel.at[1], ssem.at[1], rsem.at[1], up),
            rcopy(outs.at[up], ins.at[q], ssem.at[2], rsem.at[2], up),
            rcopy(outs.at[dn], ins.at[q], ssem.at[3], rsem.at[3], dn),
            rcopy(rel.at[0], far_ins[0], ssem.at[4], rsem.at[4], dn),
            rcopy(rel.at[1], far_ins[1], ssem.at[5], rsem.at[5], up),
        ]

    def begin(copies, own_copy):
        for copy in copies[:4]:
            copy.start()
        own_copy.start()

    def forward(copies):
        copies[0].wait_recv()
        copies[4].start()
        copies[1].wait_recv()
        copies[5].start()

    def finish(copies, own_copy):
        for copy in copies[2:]:
            copy.wait_recv()
        own_copy.wait()

    def window(t):
        return pl.ds(pl.multiple_of(LANES * (t + t // 2), LANES), 2 * LANES)

    roots = exchange(
        [ro.at[opp, n, :, window(q)] for n in range(2)], ro, ri,
        [ri.at[up, 0, :, window(up)], ri.at[dn, 1, :, window(dn)]], rrel, ro_s, ro_r,
    )
    roots_own = pltpu.make_async_copy(ro.at[q], ri.at[q], copy_sem.at[0])

    first_sends(0)
    greet(near_sem, near)
    first_sends(1)
    pl.semaphore_wait(near_sem, len(near))
    greet(line_sem, further)
    loads[1].wait()
    loads[2].wait()
    for t in range(4):
        slot = stbl[lax.rem(t + 4 - my_shift, 4)]
        ro[t, 0] = rl_v[slot]
        ro[t, 1] = rr_v[slot]
    pl.semaphore_wait(line_sem, len(further))
    greet(plane_sem, x_line)
    relay_sums(0)
    first_sends(2)
    pl.semaphore_wait(plane_sem, len(x_line))
    greet(cube_sem, y_line)
    relay_sums(1)
    full_sums(0)
    pl.semaphore_wait(cube_sem, len(y_line))
    send_pieces(0)
    relay_sums(2)
    begin(roots, roots_own)
    full_sums(1)
    send_pieces(1)
    full_sums(2)
    send_pieces(2)
    forward(roots)
    finish(roots, roots_own)
    for n in range(2):
        turned[...] = ri[:, n, :, window(opp)].reshape(block, 2 * LANES).T
        ri[opp, n] = turned[pl.ds(pl.multiple_of(64 * lax.rem(opp, 2), 16), band), :]

    for n in range(3):
        await_block(a_r, n)

    def unpack_block(k, carry):
        c = lax.rem(k, 2)
        row0 = pl.multiple_of(k * TALL, 16)
        for t in range(4):
            G[pl.ds(row0, TALL), t * LANES : (t + 1) * LANES] = gi[t, k, 0:TALL, :]
        for t in range(2):
            into = slice((4 + t) * LANES, (5 + t) * LANES)
            G[pl.ds(row0, 32), into] = gi[t + 2 * c, k, TALL:PIECE, :]
            G[pl.ds(pl.multiple_of(row0 + 32, 16), 16), into] = gi[t + 2 * (1 - c), k, TALL:64, :]
        return carry

    lax.fori_loop(0, group, unpack_block, 0)

    per_band = band // TALL

    def precondition(b, carry):
        p = jnp.dot(ri[b, 0], G[...], preferred_element_type=F32).astype(BF16)
        u = jnp.dot(p, ri[:, 1].reshape(block, block), preferred_element_type=F32).astype(BF16)
        for n in range(per_band):
            k = b * per_band + n
            row0, c = n * TALL, n % 2
            for t in range(4):
                uo[t, k, 0:TALL, :] = u[row0 : row0 + TALL, t * LANES : (t + 1) * LANES]
            for t in range(2):
                part = u[row0 : row0 + TALL, (4 + t) * LANES : (5 + t) * LANES]
                uo[t + 2 * c, k, TALL:PIECE, :] = part[0:32]
                uo[t + 2 * (1 - c), k, TALL:64, :] = part[32:TALL]
        return carry

    lax.fori_loop(0, 4, precondition, 0)

    rb = (rb0, rb1, rb2)

    def send_back(n):
        row, count = CHUNKS[n]
        rows = pl.ds(row, count)

        def one(e, carry):
            if n < 2:
                t, k = lax.rem(e, 4), lax.rem(e // 4 + fk, group)
            else:
                k = lax.rem(e // 2 + fk, group)
                t = 2 * lax.rem(k, 2) + lax.rem(e, 2)
            p = site_row * group + k
            copy = pltpu.make_async_remote_copy(
                src_ref=uo.at[t, k, rows], dst_ref=rb[n].at[f], send_sem=b_s.at[n], recv_sem=b_r.at[n],
                device_id=(p, t), device_id_type=MESH,
            )

            @pl.when(jnp.logical_not(jnp.logical_and(p == f, t == q)))
            def _():
                copy.start()

            return carry

        lax.fori_loop(0, nf if n < 2 else nf // 2, one, 0)

        @pl.when(own_row)
        def _():
            rb[n][f] = uo[q, fk, row : row + count]

    for n in range(3):
        send_back(n)

    GT[...] = G[...].T

    def products_left(c, carry):
        rows = G[pl.ds(pl.multiple_of(c * band, 16), band), :]
        to[c, 0] = lax.dot_general(
            rows, G[...], (((1,), (1,)), ((), ())), preferred_element_type=F32
        ).astype(BF16)
        return carry

    def products_right(c, carry):
        rows = GT[pl.ds(pl.multiple_of(c * band, 16), band), :]
        to[c, 1] = jnp.dot(rows, G[...], preferred_element_type=F32).astype(BF16)
        return carry

    lax.fori_loop(0, 4, products_left, 0)
    lax.fori_loop(0, 4, products_right, 0)

    stats = exchange(
        [to.at[opp, 0], to.at[opp, 1]], to, ti, [ti.at[up, 0], ti.at[dn, 1]], trel, t_s, t_r
    )
    stats_own = pltpu.make_async_copy(to.at[q], ti.at[q], copy_sem.at[1])
    begin(stats, stats_own)
    forward(stats)

    def spread(n):
        row, count = CHUNKS[n]
        lo, hi, rows = pl.ds(0, half), pl.ds(half, half), pl.ds(row, count)
        if n < 2:
            t_q = t_up = t_dn = t_opp = None
        else:
            t_q, t_up, t_dn, t_opp = tall_q, tall_up, tall_dn, tall_opp
        ss, rr = ag_s.at[n], ag_r.at[n]
        mine = ag.at[q, :, rows]
        from_up, from_dn = ag.at[up, lo, rows], ag.at[dn, hi, rows]
        return [
            rcopy(mine, mine, ss.at[0], rr.at[0], up, t_q, t_dn),
            rcopy(mine, mine, ss.at[1], rr.at[1], dn, t_q, t_up),
            rcopy(from_up, from_up, ss.at[2], rr.at[2], dn, t_up, t_opp),
            rcopy(from_dn, from_dn, ss.at[3], rr.at[3], up, t_dn, t_opp),
        ]

    gather = [spread(n) for n in range(3)]

    def start_gather(n):
        row, count = CHUNKS[n]
        await_strip(b_r, n)

        def pick(j, carry):
            ag[q, j, row : row + count] = rb[n][own[fi, j]]
            return carry

        lax.fori_loop(0, bcols, pick, 0)
        gather[n][0].start()
        gather[n][1].start()

    def forward_gather(n):
        gather[n][1].wait_recv()
        gather[n][2].start()
        gather[n][0].wait_recv()
        gather[n][3].start()

    start_gather(0)
    start_gather(1)
    forward_gather(0)
    start_gather(2)
    forward_gather(1)
    forward_gather(2)

    finish(stats, stats_own)
    loads[3].wait()
    loads[4].wait()
    for s in range(slots):
        for n, ref in ((0, sl_v), (1, sr_v)):
            old = ref[s]
            term = ti[lax.rem(slot_row[s] + my_shift, 4), n].astype(F32)
            ref[s] = jnp.where(slot_valid[s] > 0, stat_decay * old + (1.0 - stat_decay) * term, old)
    stores = [
        pltpu.make_async_copy(sl_v, nl_hbm, store_sem.at[0]),
        pltpu.make_async_copy(sr_v, nr_hbm, store_sem.at[1]),
    ] + [
        pltpu.make_async_copy(up_v.at[pl.ds(row, 16)], up_hbm.at[pl.ds(row, 16)], store_sem.at[2 + n])
        for n, row in enumerate((0, 32, 16))
    ]
    stores[0].start()
    stores[1].start()

    def finish_gather(n):
        gather[n][2].wait_recv()
        gather[n][3].wait_recv()

        def unpack_row(j, carry):
            base = j * block
            if n == 0:
                for t in range(4):
                    up_v[0:32, lanes(base, t)] = ag[t, j, 0:32, :]
            elif n == 1:
                for t in range(4):
                    up_v[32:TALL, lanes(base, t)] = ag[t, j, 32:TALL, :]
                for t in range(2):
                    up_v[0:16, lanes(base, 4 + t)] = ag[t + 2 * core, j, TALL:64, :]
                    up_v[32:TALL, lanes(base, 4 + t)] = ag[t + 2 * (1 - core), j, TALL:64, :]
            else:
                for t in range(2):
                    up_v[16:32, lanes(base, 4 + t)] = ag[t + 2 * core, j, 64:PIECE, :]
            return carry

        lax.fori_loop(0, bcols, unpack_row, 0)

    finish_gather(0)
    finish_gather(1)
    stores[2].start()
    stores[3].start()
    finish_gather(2)
    stores[4].start()

    for copies in rs + [roots, stats] + gather:
        for copy in copies:
            copy.wait_send()
    for n in range(3):
        await_strip(a_s, n)
        await_block(b_s, n)
    for store in stores:
        store.wait()


def shards(grads, owner_map, stats_left, stats_right, roots_left, roots_right):
    _, rows, width = grads.shape
    slots, band, block = stats_left.shape
    brows, bcols = owner_map.shape
    nf = lax.axis_size("fsdp")
    group = nf // brows
    half = bcols // 2
    dma, count, reg = pltpu.SemaphoreType.DMA, pltpu.SemaphoreType.REGULAR, pltpu.VMEM
    msg = (PIECE, LANES)
    scratch = [
        reg((rows, width), BF16),
        reg((4, bcols) + msg, BF16),
        reg((2, half) + msg, BF16),
        reg((2, half) + msg, BF16),
        reg((2, half) + msg, BF16),
        reg((2, half) + msg, BF16),
        reg((bcols,) + msg, BF16),
        reg((nf,) + msg, BF16),
        reg((4, 2, band, block), BF16),
        reg((4, 2, band, block), BF16),
        reg((2, band, 2 * LANES), BF16),
        reg((2 * LANES, block), BF16),
        reg((4, group) + msg, BF16),
        reg((block, block), BF16),
        reg((block, block), BF16),
        reg((4, group) + msg, BF16),
        reg((nf, 32, LANES), BF16),
        reg((nf, 32, LANES), BF16),
        reg((nf, 16, LANES), BF16),
        reg((4, bcols) + msg, BF16),
        reg((4, 2, band, block), BF16),
        reg((4, 2, band, block), BF16),
        reg((2, band, block), BF16),
        reg((slots, band, block), F32),
        reg((slots, band, block), F32),
        reg((slots, band, block), BF16),
        reg((slots, band, block), BF16),
        reg((rows, width), BF16),
        pltpu.SMEM((nf,), jnp.int32),
        pltpu.SMEM((brows,), jnp.int32),
        dma((5,)), dma((2,)), dma((5,)), count, count, count, count,
        dma((3, 6)), dma((3, 6)), dma((3,)), dma((3,)), dma((6,)), dma((6,)),
        dma((3,)), dma((3,)), dma((6,)), dma((6,)), dma((3, 4)), dma((3, 4)),
    ]
    hbm = pl.BlockSpec(memory_space=pl.ANY)
    return pl.pallas_call(
        kernel,
        out_shape=(
            jax.ShapeDtypeStruct(stats_left.shape, F32),
            jax.ShapeDtypeStruct(stats_right.shape, F32),
            jax.ShapeDtypeStruct((rows, width), BF16),
        ),
        in_specs=[pl.BlockSpec(memory_space=pltpu.SMEM)] + [hbm] * 5,
        out_specs=(hbm, hbm, hbm),
        scratch_shapes=scratch,
        compiler_params=pltpu.CompilerParams(
            collective_id=0, has_side_effects=True, vmem_limit_bytes=60 * 1024 * 1024
        ),
        name="shampoo",
    )(owner_map, grads, stats_left, stats_right, roots_left, roots_right)


def solution(mesh):
    in_specs = (
        P("rep", "fsdp", None),
        P(),
        P("fsdp", "rep", None),
        P("fsdp", "rep", None),
        P("fsdp", "rep", None),
        P("fsdp", "rep", None),
    )
    out_specs = (P("fsdp", "rep", None), P("fsdp", "rep", None), P("fsdp", None))
    return jax.shard_map(shards, mesh=mesh, in_specs=in_specs, out_specs=out_specs, check_vma=False)
```

time: 140 us -> 126 us (0.900)
  Pallas kernels: 132 us -> 118 us
    pallas_call x1, Pallas kernels: 132 us -> 118 us  [shards(): pl.pallas_call(kernel, out_shape=(jax.ShapeDtypeStruct(stats_left.shape,...]
where the time goes in v2:
time: 126 us; the launch traced here: 125 us
  Pallas kernels  118 us (94%)
  local copies, waits for them, and re-layouts  6.25 us (5%)
    pallas_call x1, Pallas kernels, shards(): pl.pallas_call(kernel, out_shape=(jax.ShapeDtypeStruct(stats_left.shape,...  118 us
    unnamed x7, local copies, waits for them, and re-layouts  6.25 us

profile of v2, /device:TPU:1, one launch (start us, length us, event | category | flops | bytes accessed | tf_op | source)
XLA Modules:
  0.0 125.3 jit_solution(10700064639181372238)
XLA Ops:
  0.6 118.4 %shampoo.1 = (f32[3,192,768]{2,1,0:T(8,128)}, f32[3,192,768]{2,1,0:T(8,128)}, bf16[48,18432]{1,0:T(8,128)(2,1)}) custom-call(s32[4,24]{1,0:T(4,128)} %own.1, bf16[1,48,18432]{2,1,0:T(8,128)(2,1)} %g_hbm.1, f32[3,192,768]{2,1,0:T(8,128)} %sl_hbm.1, f32[3,192,768]{2,1,0:T(8,128)} %sr_hbm.1, bf16[3,192,768]{2,1,0:T(8,128)(2,1)} %rl_hbm.1, ...), custom_call_target="tpu_custom_call" | custom-call | tf_op jit(solution)/shard_map/shampoo/pallas_call | solution.py:562
  119.1 0.0 copy-start.1
  119.1 2.9 %copy.12 = f32[3,192,768]{2,1,0:T(8,128)} copy(f32[3,192,768]{2,1,0:T(8,128)} %get-tuple-element.6) | data formatting | bytes 3538944
  122.0 0.0 copy-done.1
  122.0 0.0 copy-start
  122.0 1.2 copy.13
  123.2 0.9 copy-done
  124.1 1.2 copy.14
Async XLA Ops:
  119.1 2.9 %copy-start.1 = (f32[3,192,768]{2,1,0:T(8,128)S(1)}, f32[3,192,768]{2,1,0:T(8,128)}, u32[]{:S(2)}) copy-start(f32[3,192,768]{2,1,0:T(8,128)} %get-tuple-element.7) | copy-start | bytes 5308420
  122.0 2.1 %copy-start = (bf16[48,18432]{1,0:T(8,128)(2,1)S(1)}, bf16[48,18432]{1,0:T(8,128)(2,1)}, u32[]{:S(2)}) copy-start(bf16[48,18432]{1,0:T(8,128)(2,1)} %get-tuple-element.8) | copy-start | bytes 5308420

commit v3 on v2

--- a/solution.py
+++ b/solution.py
@@ -40,12 +40,12 @@
 
 
 def kernel(
-    own, g_hbm, sl_hbm, sr_hbm, rl_hbm, rr_hbm,
-    nl_hbm, nr_hbm, up_hbm,
+    own, g_hbm, rl_hbm, rr_hbm,
+    decay, terms_hbm, up_hbm,
     g_v, pk, rs_rel, rs_dir, rs_acc, rs_out, strip,
-    out, ro, ri, rrel, turned, gi, G, GT,
-    uo, rb0, rb1, rb2, ag, to, ti, trel,
-    sl_v, sr_v, rl_v, rr_v, up_v, jtbl, stbl,
+    out, ro, ri, turned, gi, G, GT,
+    uo, rb0, rb1, rb2, ag, to, ti, terms,
+    rl_v, rr_v, up_v, jtbl, stbl,
     load_sem, copy_sem, store_sem, near_sem, line_sem, plane_sem, cube_sem,
     rs_s, rs_r, a_s, a_r, ro_s, ro_r, b_s, b_r, t_s, t_r, ag_s, ag_r,
 ):
@@ -55,7 +55,7 @@
     brows, bcols = own.shape
     group = nf // brows
     block = G.shape[0]
-    slots, band, _ = sl_v.shape
+    slots, band, _ = rl_v.shape
     half = bcols // 2
     up, dn, opp = lax.rem(q + 1, 4), lax.rem(q + 3, 4), lax.rem(q + 2, 4)
     fi, fk, core = f // group, lax.rem(f, group), lax.rem(f, 2)
@@ -70,7 +70,7 @@
     loads = [
         pltpu.make_async_copy(src, dst, load_sem.at[n])
         for n, (src, dst) in enumerate(
-            [(g_hbm.at[0], g_v), (rl_hbm, rl_v), (rr_hbm, rr_v), (sl_hbm, sl_v), (sr_hbm, sr_v)]
+            [(g_hbm.at[0], g_v), (rl_hbm, rl_v), (rr_hbm, rr_v)]
         )
     ]
 
@@ -254,39 +254,20 @@
         else:
             await_pieces(sem, n, nf // 2, jnp.logical_and(own_row, tall_q))
 
-    def exchange(far, outs, ins, far_ins, rel, ssem, rsem):
-        return [
-            rcopy(far[0], rel.at[0], ssem.at[0], rsem.at[0], dn),
-            rcopy(far[1], rel.at[1], ssem.at[1], rsem.at[1], up),
-            rcopy(outs.at[up], ins.at[q], ssem.at[2], rsem.at[2], up),
-            rcopy(outs.at[dn], ins.at[q], ssem.at[3], rsem.at[3], dn),
-            rcopy(rel.at[0], far_ins[0], ssem.at[4], rsem.at[4], dn),
-            rcopy(rel.at[1], far_ins[1], ssem.at[5], rsem.at[5], up),
-        ]
-
-    def begin(copies, own_copy):
-        for copy in copies[:4]:
-            copy.start()
-        own_copy.start()
-
-    def forward(copies):
-        copies[0].wait_recv()
-        copies[4].start()
-        copies[1].wait_recv()
-        copies[5].start()
-
-    def finish(copies, own_copy):
-        for copy in copies[2:]:
+    def await_all(copies, own_copy):
+        for copy in copies:
             copy.wait_recv()
         own_copy.wait()
 
     def window(t):
         return pl.ds(pl.multiple_of(LANES * (t + t // 2), LANES), 2 * LANES)
 
-    roots = exchange(
-        [ro.at[opp, n, :, window(q)] for n in range(2)], ro, ri,
-        [ri.at[up, 0, :, window(up)], ri.at[dn, 1, :, window(dn)]], rrel, ro_s, ro_r,
-    )
+    far_out, far_in = ro.at[opp, :, :, window(q)], ri.at[q, :, :, window(q)]
+    roots = [
+        rcopy(far_out, far_in, ro_s.at[0], ro_r.at[0], opp),
+        rcopy(ro.at[up], ri.at[q], ro_s.at[1], ro_r.at[1], up),
+        rcopy(ro.at[dn], ri.at[q], ro_s.at[2], ro_r.at[2], dn),
+    ]
     roots_own = pltpu.make_async_copy(ro.at[q], ri.at[q], copy_sem.at[0])
 
     first_sends(0)
@@ -311,13 +292,14 @@
     pl.semaphore_wait(cube_sem, len(y_line))
     send_pieces(0)
     relay_sums(2)
-    begin(roots, roots_own)
+    for copy in roots:
+        copy.start()
+    roots_own.start()
     full_sums(1)
     send_pieces(1)
     full_sums(2)
     send_pieces(2)
-    forward(roots)
-    finish(roots, roots_own)
+    await_all(roots, roots_own)
     for n in range(2):
         turned[...] = ri[:, n, :, window(opp)].reshape(block, 2 * LANES).T
         ri[opp, n] = turned[pl.ds(pl.multiple_of(64 * lax.rem(opp, 2), 16), band), :]
@@ -337,6 +319,40 @@
         return carry
 
     lax.fori_loop(0, group, unpack_block, 0)
+
+    def exchange(n):
+        ss, rr = t_s.at[n], t_r.at[n]
+        return [
+            rcopy(to.at[n, opp], ti.at[n, q], ss.at[0], rr.at[0], opp),
+            rcopy(to.at[n, up], ti.at[n, q], ss.at[1], rr.at[1], up),
+            rcopy(to.at[n, dn], ti.at[n, q], ss.at[2], rr.at[2], dn),
+        ], pltpu.make_async_copy(to.at[n, q], ti.at[n, q], copy_sem.at[1 + n])
+
+    def products_left(c, carry):
+        rows = G[pl.ds(pl.multiple_of(c * band, 16), band), :]
+        to[0, c] = lax.dot_general(
+            rows, G[...], (((1,), (1,)), ((), ())), preferred_element_type=F32
+        ).astype(BF16)
+        return carry
+
+    def products_right(c, carry):
+        rows = GT[pl.ds(pl.multiple_of(c * band, 16), band), :]
+        to[1, c] = jnp.dot(rows, G[...], preferred_element_type=F32).astype(BF16)
+        return carry
+
+    stats = [exchange(n) for n in range(2)]
+
+    def send_products(n):
+        copies, own_copy = stats[n]
+        for copy in copies:
+            copy.start()
+        own_copy.start()
+
+    lax.fori_loop(0, 4, products_left, 0)
+    send_products(0)
+    GT[...] = G[...].T
+    lax.fori_loop(0, 4, products_right, 0)
+    send_products(1)
 
     per_band = band // TALL
 
@@ -388,30 +404,6 @@
 
     for n in range(3):
         send_back(n)
-
-    GT[...] = G[...].T
-
-    def products_left(c, carry):
-        rows = G[pl.ds(pl.multiple_of(c * band, 16), band), :]
-        to[c, 0] = lax.dot_general(
-            rows, G[...], (((1,), (1,)), ((), ())), preferred_element_type=F32
-        ).astype(BF16)
-        return carry
-
-    def products_right(c, carry):
-        rows = GT[pl.ds(pl.multiple_of(c * band, 16), band), :]
-        to[c, 1] = jnp.dot(rows, G[...], preferred_element_type=F32).astype(BF16)
-        return carry
-
-    lax.fori_loop(0, 4, products_left, 0)
-    lax.fori_loop(0, 4, products_right, 0)
-
-    stats = exchange(
-        [to.at[opp, 0], to.at[opp, 1]], to, ti, [ti.at[up, 0], ti.at[dn, 1]], trel, t_s, t_r
-    )
-    stats_own = pltpu.make_async_copy(to.at[q], ti.at[q], copy_sem.at[1])
-    begin(stats, stats_own)
-    forward(stats)
 
     def spread(n):
         row, count = CHUNKS[n]
@@ -457,23 +449,18 @@
     forward_gather(1)
     forward_gather(2)
 
-    finish(stats, stats_own)
-    loads[3].wait()
-    loads[4].wait()
+    for copies, own_copy in stats:
+        await_all(copies, own_copy)
     for s in range(slots):
-        for n, ref in ((0, sl_v), (1, sr_v)):
-            old = ref[s]
-            term = ti[lax.rem(slot_row[s] + my_shift, 4), n].astype(F32)
-            ref[s] = jnp.where(slot_valid[s] > 0, stat_decay * old + (1.0 - stat_decay) * term, old)
-    stores = [
-        pltpu.make_async_copy(sl_v, nl_hbm, store_sem.at[0]),
-        pltpu.make_async_copy(sr_v, nr_hbm, store_sem.at[1]),
-    ] + [
-        pltpu.make_async_copy(up_v.at[pl.ds(row, 16)], up_hbm.at[pl.ds(row, 16)], store_sem.at[2 + n])
+        decay[s] = jnp.where(slot_valid[s] > 0, jnp.float32(stat_decay), jnp.float32(1.0))
+        for n in range(2):
+            term = ti[n, lax.rem(slot_row[s] + my_shift, 4)]
+            terms[n, s] = jnp.where(slot_valid[s] > 0, term, jnp.zeros_like(term))
+    stores = [pltpu.make_async_copy(terms, terms_hbm, store_sem.at[0])] + [
+        pltpu.make_async_copy(up_v.at[pl.ds(row, 16)], up_hbm.at[pl.ds(row, 16)], store_sem.at[1 + n])
         for n, row in enumerate((0, 32, 16))
     ]
     stores[0].start()
-    stores[1].start()
 
     def finish_gather(n):
         gather[n][2].wait_recv()
@@ -499,12 +486,12 @@
 
     finish_gather(0)
     finish_gather(1)
+    stores[1].start()
     stores[2].start()
+    finish_gather(2)
     stores[3].start()
-    finish_gather(2)
-    stores[4].start()
-
-    for copies in rs + [roots, stats] + gather:
+
+    for copies in rs + [roots, stats[0][0], stats[1][0]] + gather:
         for copy in copies:
             copy.wait_send()
     for n in range(3):
@@ -534,7 +521,6 @@
         reg((nf,) + msg, BF16),
         reg((4, 2, band, block), BF16),
         reg((4, 2, band, block), BF16),
-        reg((2, band, 2 * LANES), BF16),
         reg((2 * LANES, block), BF16),
         reg((4, group) + msg, BF16),
         reg((block, block), BF16),
@@ -544,36 +530,38 @@
         reg((nf, 32, LANES), BF16),
         reg((nf, 16, LANES), BF16),
         reg((4, bcols) + msg, BF16),
-        reg((4, 2, band, block), BF16),
-        reg((4, 2, band, block), BF16),
-        reg((2, band, block), BF16),
-        reg((slots, band, block), F32),
-        reg((slots, band, block), F32),
+        reg((2, 4, band, block), BF16),
+        reg((2, 4, band, block), BF16),
+        reg((2, slots, band, block), BF16),
         reg((slots, band, block), BF16),
         reg((slots, band, block), BF16),
         reg((rows, width), BF16),
         pltpu.SMEM((nf,), jnp.int32),
         pltpu.SMEM((brows,), jnp.int32),
-        dma((5,)), dma((2,)), dma((5,)), count, count, count, count,
-        dma((3, 6)), dma((3, 6)), dma((3,)), dma((3,)), dma((6,)), dma((6,)),
-        dma((3,)), dma((3,)), dma((6,)), dma((6,)), dma((3, 4)), dma((3, 4)),
+        dma((3,)), dma((3,)), dma((4,)), count, count, count, count,
+        dma((3, 6)), dma((3, 6)), dma((3,)), dma((3,)), dma((3,)), dma((3,)),
+        dma((3,)), dma((3,)), dma((2, 3)), dma((2, 3)), dma((3, 4)), dma((3, 4)),
     ]
     hbm = pl.BlockSpec(memory_space=pl.ANY)
-    return pl.pallas_call(
+    decay, terms, update = pl.pallas_call(
         kernel,
         out_shape=(
-            jax.ShapeDtypeStruct(stats_left.shape, F32),
-            jax.ShapeDtypeStruct(stats_right.shape, F32),
+            jax.ShapeDtypeStruct((slots,), F32),
+            jax.ShapeDtypeStruct((2, slots, band, block), BF16),
             jax.ShapeDtypeStruct((rows, width), BF16),
         ),
-        in_specs=[pl.BlockSpec(memory_space=pltpu.SMEM)] + [hbm] * 5,
-        out_specs=(hbm, hbm, hbm),
+        in_specs=[pl.BlockSpec(memory_space=pltpu.SMEM)] + [hbm] * 3,
+        out_specs=(pl.BlockSpec(memory_space=pltpu.SMEM), hbm, hbm),
         scratch_shapes=scratch,
         compiler_params=pltpu.CompilerParams(
             collective_id=0, has_side_effects=True, vmem_limit_bytes=60 * 1024 * 1024
         ),
         name="shampoo",
-    )(owner_map, grads, stats_left, stats_right, roots_left, roots_right)
+    )(owner_map, grads, roots_left, roots_right)
+    keep = decay[:, None, None]
+    new_left = keep * stats_left + (1.0 - stat_decay) * terms[0].astype(F32)
+    new_right = keep * stats_right + (1.0 - stat_decay) * terms[1].astype(F32)
+    return new_left, new_right, update
 
 
 def solution(mesh):

time: 126 us -> 123 us (0.976)
  local copies, waits for them, and re-layouts: 6.25 us -> 1.22 us
  other arithmetic: 0 us -> 3.91 us
    unnamed x7, local copies, waits for them, and re-layouts: 6.25 us -> 1.22 us
    add x0 -> x1, other arithmetic: none -> 3.91 us  [shards(): new_right = keep * stats_right + (1.0 - stat_decay) * terms[1].astype(F32)]
where the time goes in v3:
time: 123 us
  Pallas kernels  117 us (95%)
  other arithmetic  3.91 us (3%)
    pallas_call x1, Pallas kernels, shards(): pl.pallas_call(kernel, out_shape=(jax.ShapeDtypeStruct((slots,), F32), ja...  117 us
    add x1, other arithmetic, shards(): new_right = keep * stats_right + (1.0 - stat_decay) * terms[1].astype(F32)  3.91 us

profile of v3, /device:TPU:1, one launch (start us, length us, event | category | flops | bytes accessed | tf_op | source)
XLA Modules:
  0.0 123.1 jit_solution(4047069103098489743)
XLA Ops:
  0.6 0.0 copy-start.1
  0.6 0.0 copy-start.2
  0.7 117.3 %shampoo.1 = (f32[3]{0:T(128)}, bf16[2,3,192,768]{3,2,1,0:T(8,128)(2,1)}, bf16[48,18432]{1,0:T(8,128)(2,1)}) custom-call(s32[4,24]{1,0:T(4,128)} %own.1, bf16[1,48,18432]{2,1,0:T(8,128)(2,1)} %g_hbm.1, bf16[3,192,768]{2,1,0:T(8,128)(2,1)} %rl_hbm.1, bf16[3,192,768]{2,1,0:T(8,128)(2,1)} %rr_hbm.1), custom_call_target="tpu_custom_call" | custom-call | tf_op jit(solution)/shard_map/shampoo/pallas_call | solution.py:546
  118.0 0.0 copy-done.1
  118.0 0.0 copy-done.2
  118.0 0.0 copy-start
  118.0 3.9 %bitcast_add_fusion = (f32[3,192,768]{2,1,0:T(8,128)}, f32[3,192,768]{2,1,0:T(8,128)}) fusion(f32[3,192,768]{2,1,0:T(8,128)S(1)} %copy-done.1, bf16[2,3,192,768]{3,2,1,0:T(8,128)(2,1)} %get-tuple-element.7, f32[3]{0:T(128)} %get-tuple-element.6, f32[3,192,768]{2,1,0:T(8,128)S(1)} %copy-done.2), kind=kLoop, calls=%fused_computation | loop fusion | flops 3538944 | bytes 8847372 | tf_op jit(solution)/shard_map/add | solution.py:563
  121.9 0.0 copy-done
  121.9 1.2 copy.10
Async XLA Ops:
  0.6 117.4 %copy-start.1 = (f32[3,192,768]{2,1,0:T(8,128)S(1)}, f32[3,192,768]{2,1,0:T(8,128)}, u32[]{:S(2)}) copy-start(f32[3,192,768]{2,1,0:T(8,128)} %param.9) | copy-start | bytes 5308420
  0.6 117.4 %copy-start.2 = (f32[3,192,768]{2,1,0:T(8,128)S(1)}, f32[3,192,768]{2,1,0:T(8,128)}, u32[]{:S(2)}) copy-start(f32[3,192,768]{2,1,0:T(8,128)} %param.8) | copy-start | bytes 5308420
  118.0 3.9 %copy-start = (bf16[48,18432]{1,0:T(8,128)(2,1)S(1)}, bf16[48,18432]{1,0:T(8,128)(2,1)}, u32[]{:S(2)}) copy-start(bf16[48,18432]{1,0:T(8,128)(2,1)} %get-tuple-element.16) | copy-start | bytes 5308420

commit v4 on v3

--- a/solution.py
+++ b/solution.py
@@ -11,6 +11,7 @@
 TALL = 48
 PIECE = 80
 CHUNKS = ((0, 32), (32, 32), (64, 16))
+LAST = len(CHUNKS) - 1
 BF16 = jnp.bfloat16
 F32 = jnp.float32
 
@@ -157,7 +158,7 @@
     def sums(n):
         row, count = CHUNKS[n]
         lo, hi, rows = pl.ds(0, half), pl.ds(half, half), pl.ds(row, count)
-        if n < 2:
+        if n < LAST:
             s_up = s_dn = s_opp = r_up = r_dn = r_q = None
         else:
             s_up, s_dn, s_opp, r_up, r_dn, r_q = tall_up, tall_dn, tall_opp, tall_up, tall_dn, tall_q
@@ -171,7 +172,7 @@
             rcopy(rs_out.at[1, :, rows], rs_acc.at[1, :, rows], ss.at[5], rr.at[5], up, s_up, r_q),
         ]
 
-    rs = [sums(n) for n in range(3)]
+    rs = [sums(n) for n in range(len(CHUNKS))]
 
     def first_sends(n):
         for copy in rs[n][:4]:
@@ -233,7 +234,7 @@
                 out[f, row : row + count] = strip[jtbl[f], row : row + count]
                 piece_copy(f).start()
 
-        gated(None if n < 2 else tall_q, send_all)
+        gated(None if n < LAST else tall_q, send_all)
 
     def await_pieces(sem, n, total, here):
         count = CHUNKS[n][1]
@@ -246,10 +247,10 @@
         pl.when(jnp.logical_not(here))(lambda: some(total))
 
     def await_strip(sem, n):
-        gated(None if n < 2 else tall_q, lambda: await_pieces(sem, n, nf, own_row))
+        gated(None if n < LAST else tall_q, lambda: await_pieces(sem, n, nf, own_row))
 
     def await_block(sem, n):
-        if n < 2:
+        if n < LAST:
             await_pieces(sem, n, nf, own_row)
         else:
             await_pieces(sem, n, nf // 2, jnp.logical_and(own_row, tall_q))
@@ -262,13 +263,36 @@
     def window(t):
         return pl.ds(pl.multiple_of(LANES * (t + t // 2), LANES), 2 * LANES)
 
+    def inner(t):
+        return (3 * t + 1) // 2
+
+    def inner_rows(t):
+        return pl.ds(pl.multiple_of(64 * lax.rem(t, 2), 16), LANES)
+
+    def differs(m, t, u):
+        return jnp.logical_and(inner(t) != m, inner(u) != m)
+
     far_out, far_in = ro.at[opp, :, :, window(q)], ri.at[q, :, :, window(q)]
-    roots = [
-        rcopy(far_out, far_in, ro_s.at[0], ro_r.at[0], opp),
-        rcopy(ro.at[up], ri.at[q], ro_s.at[1], ro_r.at[1], up),
-        rcopy(ro.at[dn], ri.at[q], ro_s.at[2], ro_r.at[2], dn),
-    ]
+    roots = [rcopy(far_out, far_in, ro_s.at[0], ro_r.at[0], opp)]
+    for n, (to_rep, from_rep) in enumerate(((dn, up), (up, dn))):
+        more = lanes(0, inner(opp))
+        k = 1 + 7 * n
+        roots.append(rcopy(ro.at[to_rep, n, :, more], ri.at[q, n, :, more], ro_s.at[k], ro_r.at[k], to_rep))
+        for m in range(block // LANES):
+            cols = pl.ds(m * LANES, LANES)
+            k = 2 + 7 * n + m
+            roots.append(
+                rcopy(
+                    ro.at[to_rep, :, :, cols], ri.at[q, :, :, cols], ro_s.at[k], ro_r.at[k], to_rep,
+                    differs(m, to_rep, opp), differs(m, q, to_rep),
+                )
+            )
     roots_own = pltpu.make_async_copy(ro.at[q], ri.at[q], copy_sem.at[0])
+
+    def start_roots():
+        for copy in roots:
+            copy.start()
+        roots_own.start()
 
     first_sends(0)
     greet(near_sem, near)
@@ -283,28 +307,32 @@
         ro[t, 1] = rr_v[slot]
     pl.semaphore_wait(line_sem, len(further))
     greet(plane_sem, x_line)
-    relay_sums(0)
-    first_sends(2)
-    pl.semaphore_wait(plane_sem, len(x_line))
-    greet(cube_sem, y_line)
-    relay_sums(1)
-    full_sums(0)
-    pl.semaphore_wait(cube_sem, len(y_line))
-    send_pieces(0)
-    relay_sums(2)
-    for copy in roots:
-        copy.start()
-    roots_own.start()
-    full_sums(1)
-    send_pieces(1)
-    full_sums(2)
-    send_pieces(2)
+    for n in range(LAST + 1):
+        relay_sums(n)
+        if n + 2 <= LAST:
+            first_sends(n + 2)
+        if n == 0:
+            pl.semaphore_wait(plane_sem, len(x_line))
+            greet(cube_sem, y_line)
+        if n == LAST:
+            start_roots()
+        if n >= 1:
+            full_sums(n - 1)
+            if n == 1:
+                pl.semaphore_wait(cube_sem, len(y_line))
+            send_pieces(n - 1)
+    full_sums(LAST)
+    send_pieces(LAST)
     await_all(roots, roots_own)
-    for n in range(2):
+    for n, (x, y) in enumerate(((up, dn), (dn, up))):
+        mine = lanes(0, inner(q))
+        ri[:, n, :, mine] = ri[q, n, inner_rows(q), :].T.reshape(4, band, LANES)
+        turned[:, 0:LANES] = ri[x, n, inner_rows(x), window(y)].T
+        ri[y, n, :, lanes(0, inner(x))] = turned[pl.ds(pl.multiple_of(64 * lax.rem(y, 2), 16), band), 0:LANES]
         turned[...] = ri[:, n, :, window(opp)].reshape(block, 2 * LANES).T
         ri[opp, n] = turned[pl.ds(pl.multiple_of(64 * lax.rem(opp, 2), 16), band), :]
 
-    for n in range(3):
+    for n in range(len(CHUNKS)):
         await_block(a_r, n)
 
     def unpack_block(k, carry):
@@ -350,10 +378,6 @@
 
     lax.fori_loop(0, 4, products_left, 0)
     send_products(0)
-    GT[...] = G[...].T
-    lax.fori_loop(0, 4, products_right, 0)
-    send_products(1)
-
     per_band = band // TALL
 
     def precondition(b, carry):
@@ -379,7 +403,7 @@
         rows = pl.ds(row, count)
 
         def one(e, carry):
-            if n < 2:
+            if n < LAST:
                 t, k = lax.rem(e, 4), lax.rem(e // 4 + fk, group)
             else:
                 k = lax.rem(e // 2 + fk, group)
@@ -396,19 +420,23 @@
 
             return carry
 
-        lax.fori_loop(0, nf if n < 2 else nf // 2, one, 0)
+        lax.fori_loop(0, nf if n < LAST else nf // 2, one, 0)
 
         @pl.when(own_row)
         def _():
             rb[n][f] = uo[q, fk, row : row + count]
 
-    for n in range(3):
+    for n in range(len(CHUNKS)):
         send_back(n)
 
+    GT[...] = G[...].T
+    lax.fori_loop(0, 4, products_right, 0)
+
+    send_products(1)
     def spread(n):
         row, count = CHUNKS[n]
         lo, hi, rows = pl.ds(0, half), pl.ds(half, half), pl.ds(row, count)
-        if n < 2:
+        if n < LAST:
             t_q = t_up = t_dn = t_opp = None
         else:
             t_q, t_up, t_dn, t_opp = tall_q, tall_up, tall_dn, tall_opp
@@ -422,7 +450,7 @@
             rcopy(from_dn, from_dn, ss.at[3], rr.at[3], up, t_dn, t_opp),
         ]
 
-    gather = [spread(n) for n in range(3)]
+    gather = [spread(n) for n in range(len(CHUNKS))]
 
     def start_gather(n):
         row, count = CHUNKS[n]
@@ -442,12 +470,11 @@
         gather[n][0].wait_recv()
         gather[n][3].start()
 
-    start_gather(0)
-    start_gather(1)
-    forward_gather(0)
-    start_gather(2)
-    forward_gather(1)
-    forward_gather(2)
+    for n in range(LAST + 1):
+        start_gather(n)
+        if n >= 1:
+            forward_gather(n - 1)
+    forward_gather(LAST)
 
     for copies, own_copy in stats:
         await_all(copies, own_copy)
@@ -466,35 +493,36 @@
         gather[n][2].wait_recv()
         gather[n][3].wait_recv()
 
+        row, count = CHUNKS[n]
+        end = row + count
+
         def unpack_row(j, carry):
             base = j * block
-            if n == 0:
+            if row < TALL:
+                rows = slice(row, min(end, TALL))
                 for t in range(4):
-                    up_v[0:32, lanes(base, t)] = ag[t, j, 0:32, :]
-            elif n == 1:
-                for t in range(4):
-                    up_v[32:TALL, lanes(base, t)] = ag[t, j, 32:TALL, :]
-                for t in range(2):
+                    up_v[rows, lanes(base, t)] = ag[t, j, rows, :]
+            for t in range(2):
+                if row < 64 and end > TALL:
                     up_v[0:16, lanes(base, 4 + t)] = ag[t + 2 * core, j, TALL:64, :]
                     up_v[32:TALL, lanes(base, 4 + t)] = ag[t + 2 * (1 - core), j, TALL:64, :]
-            else:
-                for t in range(2):
+                if n == LAST:
                     up_v[16:32, lanes(base, 4 + t)] = ag[t + 2 * core, j, 64:PIECE, :]
             return carry
 
         lax.fori_loop(0, bcols, unpack_row, 0)
 
-    finish_gather(0)
-    finish_gather(1)
+    for n in range(LAST):
+        finish_gather(n)
     stores[1].start()
     stores[2].start()
-    finish_gather(2)
+    finish_gather(LAST)
     stores[3].start()
 
     for copies in rs + [roots, stats[0][0], stats[1][0]] + gather:
         for copy in copies:
             copy.wait_send()
-    for n in range(3):
+    for n in range(len(CHUNKS)):
         await_strip(a_s, n)
         await_block(b_s, n)
     for store in stores:
@@ -508,7 +536,8 @@
     nf = lax.axis_size("fsdp")
     group = nf // brows
     half = bcols // 2
-    dma, count, reg = pltpu.SemaphoreType.DMA, pltpu.SemaphoreType.REGULAR, pltpu.VMEM
+    parts = len(CHUNKS)
+    dma, tally, reg = pltpu.SemaphoreType.DMA, pltpu.SemaphoreType.REGULAR, pltpu.VMEM
     msg = (PIECE, LANES)
     scratch = [
         reg((rows, width), BF16),
@@ -526,9 +555,7 @@
         reg((block, block), BF16),
         reg((block, block), BF16),
         reg((4, group) + msg, BF16),
-        reg((nf, 32, LANES), BF16),
-        reg((nf, 32, LANES), BF16),
-        reg((nf, 16, LANES), BF16),
+        *[reg((nf, count, LANES), BF16) for _, count in CHUNKS],
         reg((4, bcols) + msg, BF16),
         reg((2, 4, band, block), BF16),
         reg((2, 4, band, block), BF16),
@@ -538,9 +565,9 @@
         reg((rows, width), BF16),
         pltpu.SMEM((nf,), jnp.int32),
         pltpu.SMEM((brows,), jnp.int32),
-        dma((3,)), dma((3,)), dma((4,)), count, count, count, count,
-        dma((3, 6)), dma((3, 6)), dma((3,)), dma((3,)), dma((3,)), dma((3,)),
-        dma((3,)), dma((3,)), dma((2, 3)), dma((2, 3)), dma((3, 4)), dma((3, 4)),
+        dma((3,)), dma((3,)), dma((4,)), tally, tally, tally, tally,
+        dma((parts, 6)), dma((parts, 6)), dma((parts,)), dma((parts,)), dma((15,)), dma((15,)),
+        dma((parts,)), dma((parts,)), dma((2, 3)), dma((2, 3)), dma((parts, 4)), dma((parts, 4)),
     ]
     hbm = pl.BlockSpec(memory_space=pl.ANY)
     decay, terms, update = pl.pallas_call(

time: 123 us -> 120 us (0.976); the launches traced: 123 us -> 118 us
  Pallas kernels: 117 us -> 113 us
    pallas_call x1, Pallas kernels: 117 us -> 113 us  [shards(): pl.pallas_call(kernel, out_shape=(jax.ShapeDtypeStruct((slots,), F32), ja...]
where the time goes in v4:
time: 120 us; the launch traced here: 118 us
  Pallas kernels  113 us (94%)
  other arithmetic  3.91 us (3%)
  local copies, waits for them, and re-layouts  1.22 us (1%)
    pallas_call x1, Pallas kernels, shards(): pl.pallas_call(kernel, out_shape=(jax.ShapeDtypeStruct((slots,), F32), ja...  113 us
    add x1, other arithmetic, shards(): new_right = keep * stats_right + (1.0 - stat_decay) * terms[1].astype(F32)  3.91 us

profile of v4, /device:TPU:1, one launch (start us, length us, event | category | flops | bytes accessed | tf_op | source)
XLA Modules:
  0.0 118.4 jit_solution(9244160743782593572)
XLA Ops:
  0.6 0.0 copy-start.1
  0.6 0.0 copy-start.2
  0.7 112.6 %shampoo.1 = (f32[3]{0:T(128)}, bf16[2,3,192,768]{3,2,1,0:T(8,128)(2,1)}, bf16[48,18432]{1,0:T(8,128)(2,1)}) custom-call(s32[4,24]{1,0:T(4,128)} %own.1, bf16[1,48,18432]{2,1,0:T(8,128)(2,1)} %g_hbm.1, bf16[3,192,768]{2,1,0:T(8,128)(2,1)} %rl_hbm.1, bf16[3,192,768]{2,1,0:T(8,128)(2,1)} %rr_hbm.1), custom_call_target="tpu_custom_call" | custom-call | tf_op jit(solution)/shard_map/shampoo/pallas_call | solution.py:573
  113.3 0.0 copy-done.1
  113.3 0.0 copy-done.2
  113.3 0.0 copy-start
  113.3 3.9 %bitcast_add_fusion = (f32[3,192,768]{2,1,0:T(8,128)}, f32[3,192,768]{2,1,0:T(8,128)}) fusion(f32[3,192,768]{2,1,0:T(8,128)S(1)} %copy-done.1, bf16[2,3,192,768]{3,2,1,0:T(8,128)(2,1)} %get-tuple-element.7, f32[3]{0:T(128)} %get-tuple-element.6, f32[3,192,768]{2,1,0:T(8,128)S(1)} %copy-done.2), kind=kLoop, calls=%fused_computation | loop fusion | flops 3538944 | bytes 8847372 | tf_op jit(solution)/shard_map/add | solution.py:590
  117.2 0.0 copy-done
  117.2 1.2 %copy.10 = bf16[48,18432]{1,0:T(8,128)(2,1)} copy(bf16[48,18432]{1,0:T(8,128)(2,1)S(1)} %copy-done) | data formatting | bytes 3538944
Async XLA Ops:
  0.6 112.6 %copy-start.1 = (f32[3,192,768]{2,1,0:T(8,128)S(1)}, f32[3,192,768]{2,1,0:T(8,128)}, u32[]{:S(2)}) copy-start(f32[3,192,768]{2,1,0:T(8,128)} %param.9) | copy-start | bytes 5308420
  0.6 112.6 %copy-start.2 = (f32[3,192,768]{2,1,0:T(8,128)S(1)}, f32[3,192,768]{2,1,0:T(8,128)}, u32[]{:S(2)}) copy-start(f32[3,192,768]{2,1,0:T(8,128)} %param.8) | copy-start | bytes 5308420
  113.3 3.9 %copy-start = (bf16[48,18432]{1,0:T(8,128)(2,1)S(1)}, bf16[48,18432]{1,0:T(8,128)(2,1)}, u32[]{:S(2)}) copy-start(bf16[48,18432]{1,0:T(8,128)(2,1)} %get-tuple-element.16) | copy-start | bytes 5308420

commit v5 on v4

--- a/solution.py
+++ b/solution.py
@@ -314,8 +314,6 @@
         if n == 0:
             pl.semaphore_wait(plane_sem, len(x_line))
             greet(cube_sem, y_line)
-        if n == LAST:
-            start_roots()
         if n >= 1:
             full_sums(n - 1)
             if n == 1:
@@ -323,15 +321,7 @@
             send_pieces(n - 1)
     full_sums(LAST)
     send_pieces(LAST)
-    await_all(roots, roots_own)
-    for n, (x, y) in enumerate(((up, dn), (dn, up))):
-        mine = lanes(0, inner(q))
-        ri[:, n, :, mine] = ri[q, n, inner_rows(q), :].T.reshape(4, band, LANES)
-        turned[:, 0:LANES] = ri[x, n, inner_rows(x), window(y)].T
-        ri[y, n, :, lanes(0, inner(x))] = turned[pl.ds(pl.multiple_of(64 * lax.rem(y, 2), 16), band), 0:LANES]
-        turned[...] = ri[:, n, :, window(opp)].reshape(block, 2 * LANES).T
-        ri[opp, n] = turned[pl.ds(pl.multiple_of(64 * lax.rem(opp, 2), 16), band), :]
-
+    start_roots()
     for n in range(len(CHUNKS)):
         await_block(a_r, n)
 
@@ -378,6 +368,19 @@
 
     lax.fori_loop(0, 4, products_left, 0)
     send_products(0)
+    GT[...] = G[...].T
+    lax.fori_loop(0, 4, products_right, 0)
+
+    send_products(1)
+    await_all(roots, roots_own)
+    for n, (x, y) in enumerate(((up, dn), (dn, up))):
+        mine = lanes(0, inner(q))
+        ri[:, n, :, mine] = ri[q, n, inner_rows(q), :].T.reshape(4, band, LANES)
+        turned[:, 0:LANES] = ri[x, n, inner_rows(x), window(y)].T
+        ri[y, n, :, lanes(0, inner(x))] = turned[pl.ds(pl.multiple_of(64 * lax.rem(y, 2), 16), band), 0:LANES]
+        turned[...] = ri[:, n, :, window(opp)].reshape(block, 2 * LANES).T
+        ri[opp, n] = turned[pl.ds(pl.multiple_of(64 * lax.rem(opp, 2), 16), band), :]
+
     per_band = band // TALL
 
     def precondition(b, carry):
@@ -429,10 +432,6 @@
     for n in range(len(CHUNKS)):
         send_back(n)
 
-    GT[...] = G[...].T
-    lax.fori_loop(0, 4, products_right, 0)
-
-    send_products(1)
     def spread(n):
         row, count = CHUNKS[n]
         lo, hi, rows = pl.ds(0, half), pl.ds(half, half), pl.ds(row, count)

time: 120 us -> 117 us (0.975)
  Pallas kernels: 113 us -> 110 us
    pallas_call x1, Pallas kernels: 113 us -> 110 us  [shards(): pl.pallas_call(kernel, out_shape=(jax.ShapeDtypeStruct((slots,), F32), ja...]
where the time goes in v5:
time: 117 us; the launch traced here: 116 us
  Pallas kernels  110 us (94%)
  other arithmetic  3.91 us (3%)
  local copies, waits for them, and re-layouts  1.22 us (1%)
    pallas_call x1, Pallas kernels, shards(): pl.pallas_call(kernel, out_shape=(jax.ShapeDtypeStruct((slots,), F32), ja...  110 us
    add x1, other arithmetic, shards(): new_right = keep * stats_right + (1.0 - stat_decay) * terms[1].astype(F32)  3.91 us

profile of v5, /device:TPU:1, one launch (start us, length us, event | category | flops | bytes accessed | tf_op | source)
XLA Modules:
  0.0 116.3 jit_solution(9159815007140299090)
XLA Ops:
  0.6 0.0 copy-start.1
  0.6 0.0 copy-start.2
  0.7 110.5 %shampoo.1 = (f32[3]{0:T(128)}, bf16[2,3,192,768]{3,2,1,0:T(8,128)(2,1)}, bf16[48,18432]{1,0:T(8,128)(2,1)}) custom-call(s32[4,24]{1,0:T(4,128)} %own.1, bf16[1,48,18432]{2,1,0:T(8,128)(2,1)} %g_hbm.1, bf16[3,192,768]{2,1,0:T(8,128)(2,1)} %rl_hbm.1, bf16[3,192,768]{2,1,0:T(8,128)(2,1)} %rr_hbm.1), custom_call_target="tpu_custom_call" | custom-call | tf_op jit(solution)/shard_map/shampoo/pallas_call | solution.py:572
  111.1 0.0 copy-done.1
  111.1 0.0 copy-done.2
  111.1 0.0 copy-start
  111.2 3.9 %bitcast_add_fusion = (f32[3,192,768]{2,1,0:T(8,128)}, f32[3,192,768]{2,1,0:T(8,128)}) fusion(f32[3,192,768]{2,1,0:T(8,128)S(1)} %copy-done.1, bf16[2,3,192,768]{3,2,1,0:T(8,128)(2,1)} %get-tuple-element.7, f32[3]{0:T(128)} %get-tuple-element.6, f32[3,192,768]{2,1,0:T(8,128)S(1)} %copy-done.2), kind=kLoop, calls=%fused_computation | loop fusion | flops 3538944 | bytes 8847372 | tf_op jit(solution)/shard_map/add | solution.py:589
  115.1 0.0 copy-done
  115.1 1.2 %copy.10 = bf16[48,18432]{1,0:T(8,128)(2,1)} copy(bf16[48,18432]{1,0:T(8,128)(2,1)S(1)} %copy-done) | data formatting | bytes 3538944
Async XLA Ops:
  0.6 110.5 %copy-start.1 = (f32[3,192,768]{2,1,0:T(8,128)S(1)}, f32[3,192,768]{2,1,0:T(8,128)}, u32[]{:S(2)}) copy-start(f32[3,192,768]{2,1,0:T(8,128)} %param.9) | copy-start | bytes 5308420
  0.6 110.5 %copy-start.2 = (f32[3,192,768]{2,1,0:T(8,128)S(1)}, f32[3,192,768]{2,1,0:T(8,128)}, u32[]{:S(2)}) copy-start(f32[3,192,768]{2,1,0:T(8,128)} %param.8) | copy-start | bytes 5308420
  111.1 3.9 %copy-start = (bf16[48,18432]{1,0:T(8,128)(2,1)S(1)}, bf16[48,18432]{1,0:T(8,128)(2,1)}, u32[]{:S(2)}) copy-start(bf16[48,18432]{1,0:T(8,128)(2,1)} %get-tuple-element.16) | copy-start | bytes 5308420

commit v6 on v5

--- a/solution.py
+++ b/solution.py
@@ -272,8 +272,17 @@
     def differs(m, t, u):
         return jnp.logical_and(inner(t) != m, inner(u) != m)
 
-    far_out, far_in = ro.at[opp, :, :, window(q)], ri.at[q, :, :, window(q)]
-    roots = [rcopy(far_out, far_in, ro_s.at[0], ro_r.at[0], opp)]
+    def corner_rows(t):
+        return pl.ds(pl.multiple_of(LANES * (1 - lax.rem(t, 2)), 16), 64)
+
+    def corner_lanes(t):
+        return lanes(0, t + t // 2 + 1 - lax.rem(t, 2))
+
+    far = [(pl.ds(0, band), lanes(0, inner(q))), (corner_rows(q), corner_lanes(q))]
+    roots = [
+        rcopy(ro.at[opp, :, rows, cols], ri.at[q, :, rows, cols], ro_s.at[k], ro_r.at[k], opp)
+        for k, (rows, cols) in zip((0, 15), far)
+    ]
     for n, (to_rep, from_rep) in enumerate(((dn, up), (up, dn))):
         more = lanes(0, inner(opp))
         k = 1 + 7 * n
@@ -378,6 +387,8 @@
         ri[:, n, :, mine] = ri[q, n, inner_rows(q), :].T.reshape(4, band, LANES)
         turned[:, 0:LANES] = ri[x, n, inner_rows(x), window(y)].T
         ri[y, n, :, lanes(0, inner(x))] = turned[pl.ds(pl.multiple_of(64 * lax.rem(y, 2), 16), band), 0:LANES]
+        edge = ri[opp, n, corner_rows(opp), lanes(0, inner(opp))]
+        ri[opp, n, inner_rows(opp), corner_lanes(opp)] = jnp.concatenate([edge, edge], axis=0).T
         turned[...] = ri[:, n, :, window(opp)].reshape(block, 2 * LANES).T
         ri[opp, n] = turned[pl.ds(pl.multiple_of(64 * lax.rem(opp, 2), 16), band), :]
 
@@ -565,7 +576,7 @@
         pltpu.SMEM((nf,), jnp.int32),
         pltpu.SMEM((brows,), jnp.int32),
         dma((3,)), dma((3,)), dma((4,)), tally, tally, tally, tally,
-        dma((parts, 6)), dma((parts, 6)), dma((parts,)), dma((parts,)), dma((15,)), dma((15,)),
+        dma((parts, 6)), dma((parts, 6)), dma((parts,)), dma((parts,)), dma((16,)), dma((16,)),
         dma((parts,)), dma((parts,)), dma((2, 3)), dma((2, 3)), dma((parts, 4)), dma((parts, 4)),
     ]
     hbm = pl.BlockSpec(memory_space=pl.ANY)

time: 117 us -> 117 us (level)
  no operation moved by 1% of the time
where the time goes in v6:
time: 117 us; the launch traced here: 116 us
  Pallas kernels  111 us (95%)
  other arithmetic  3.91 us (3%)
  local copies, waits for them, and re-layouts  1.22 us (1%)
    pallas_call x1, Pallas kernels, shards(): pl.pallas_call(kernel, out_shape=(jax.ShapeDtypeStruct((slots,), F32), ja...  111 us
    add x1, other arithmetic, shards(): new_right = keep * stats_right + (1.0 - stat_decay) * terms[1].astype(F32)  3.91 us

profile of v6, /device:TPU:1, one launch (start us, length us, event | category | flops | bytes accessed | tf_op | source)
XLA Modules:
  0.0 116.3 jit_solution(16130789607674168550)
XLA Ops:
  0.6 0.0 copy-start.1
  0.6 0.0 copy-start.2
  0.7 110.5 %shampoo.1 = (f32[3]{0:T(128)}, bf16[2,3,192,768]{3,2,1,0:T(8,128)(2,1)}, bf16[48,18432]{1,0:T(8,128)(2,1)}) custom-call(s32[4,24]{1,0:T(4,128)} %own.1, bf16[1,48,18432]{2,1,0:T(8,128)(2,1)} %g_hbm.1, bf16[3,192,768]{2,1,0:T(8,128)(2,1)} %rl_hbm.1, bf16[3,192,768]{2,1,0:T(8,128)(2,1)} %rr_hbm.1), custom_call_target="tpu_custom_call" | custom-call | tf_op jit(solution)/shard_map/shampoo/pallas_call | solution.py:583
  111.2 0.0 copy-done.1
  111.2 0.0 copy-done.2
  111.2 0.0 copy-start
  111.2 3.9 %bitcast_add_fusion = (f32[3,192,768]{2,1,0:T(8,128)}, f32[3,192,768]{2,1,0:T(8,128)}) fusion(f32[3,192,768]{2,1,0:T(8,128)S(1)} %copy-done.1, bf16[2,3,192,768]{3,2,1,0:T(8,128)(2,1)} %get-tuple-element.7, f32[3]{0:T(128)} %get-tuple-element.6, f32[3,192,768]{2,1,0:T(8,128)S(1)} %copy-done.2), kind=kLoop, calls=%fused_computation | loop fusion | flops 3538944 | bytes 8847372 | tf_op jit(solution)/shard_map/add | solution.py:600
  115.1 0.0 copy-done
  115.1 1.2 %copy.10 = bf16[48,18432]{1,0:T(8,128)(2,1)} copy(bf16[48,18432]{1,0:T(8,128)(2,1)S(1)} %copy-done) | data formatting | bytes 3538944
Async XLA Ops:
  0.6 110.5 %copy-start.1 = (f32[3,192,768]{2,1,0:T(8,128)S(1)}, f32[3,192,768]{2,1,0:T(8,128)}, u32[]{:S(2)}) copy-start(f32[3,192,768]{2,1,0:T(8,128)} %param.9) | copy-start | bytes 5308420
  0.6 110.5 %copy-start.2 = (f32[3,192,768]{2,1,0:T(8,128)S(1)}, f32[3,192,768]{2,1,0:T(8,128)}, u32[]{:S(2)}) copy-start(f32[3,192,768]{2,1,0:T(8,128)} %param.8) | copy-start | bytes 5308420
  111.2 3.9 %copy-start = (bf16[48,18432]{1,0:T(8,128)(2,1)S(1)}, bf16[48,18432]{1,0:T(8,128)(2,1)}, u32[]{:S(2)}) copy-start(bf16[48,18432]{1,0:T(8,128)(2,1)} %get-tuple-element.16) | copy-start | bytes 5308420
